TPU v7x, 512 devices: a whole 4x8x8 slice. The times are simulated.
512 devices in a mesh: exp: 8 (over z), tp: 16 (over y, core), dp: 4 (over x).
Axes of the slice: x: 4, y: 8, z: 8, core: 2. Of those that a mesh axis runs over, the one named last changes fastest.
Arguments:
- tokens: bfloat16 [4096, 3072], P(('dp', 'exp', 'tp')), parts along dimension 0, may hold values from -6 to 6
- routes: int32 [4096, 2], P(('dp', 'exp')), parts along dimension 0, may hold values from 0 to 3, all different within a row; in each aligned block of 128 rows (0 to 127, 128 to 255, ...) at most 80 rows name the same one
- gates: float32 [4096, 2], P(('dp', 'exp')), parts along dimension 0, may hold values from 0.2 to 1
- w_gate: bfloat16 [8, 3072, 4096], P('exp', None, 'tp'), may hold values from -0.109375 to 0.109375
- w_up: bfloat16 [8, 3072, 4096], P('exp', None, 'tp'), may hold values from -0.109375 to 0.109375
- w_down: bfloat16 [8, 4096, 3072], P('exp', 'tp'), may hold values from -0.0625 to 0.0625
Outputs:
- mixed: bfloat16 [4096, 3072], P(('dp', 'exp', 'tp')), parts along dimension 0
There are 4 independent parts, one for each index of `dp`. A program takes and returns all parts, laid end to end along the dimension named above; an argument that names none is the same for every part. Nothing has to cross between parts.
Inputs may be any that keep to these rules, and one draw needn't show every extreme that they name: `routes`: each token names two different experts; within the 128 tokens of one index of exp (aligned blocks of rows) no expert is named by more than 80 tokens, a bound that some blocks reach.
All inputs are finite; a program needn't handle non-finite values.
Results may differ from a plain program's by a relative error of at most 0.023.
Values may be sent and summed in bfloat16 or wider, within the bound.
A program may use at most 64 MiB of HBM per device.

v0:
```python
import jax
import jax.numpy as jnp
from jax import lax
from jax.sharding import PartitionSpec as P


def local(tokens, routes, gates, w_gate, w_up, w_down):
    n_exp = lax.axis_size("exp")
    n_tp = lax.axis_size("tp")
    expert_count = min(4, n_exp)
    group_size = n_exp // expert_count
    block_rows = tokens.shape[0] * n_tp
    capacity = min(block_rows, block_rows * 10 // (4 * expert_count))
    width = tokens.shape[1]
    share = width // n_tp
    gathered = lax.all_gather(tokens, "tp", axis=0, tiled=True)
    expert_ids = lax.broadcasted_iota(jnp.int32, (1, 1, expert_count), 2)
    chosen = (routes[:, :, None] == expert_ids).astype(jnp.int32)
    member = jnp.sum(chosen, axis=1)
    before = jnp.cumsum(member, axis=0) - member
    slot_ids = lax.broadcasted_iota(jnp.int32, (1, 1, capacity), 2)
    placed = member[:, :, None] * (before[:, :, None] == slot_ids).astype(jnp.int32)
    placed_flat = placed.reshape(block_rows, expert_count * capacity)
    outgoing = lax.dot_general(
        placed_flat.astype(jnp.bfloat16),
        gathered,
        (((0,), (0,)), ((), ())),
        preferred_element_type=jnp.float32,
    ).astype(jnp.bfloat16)
    outgoing = jnp.broadcast_to(
        outgoing.reshape(expert_count, 1, capacity, width),
        (expert_count, group_size, capacity, width),
    )
    outgoing = outgoing.reshape(n_exp, capacity, width)
    arrived = lax.all_to_all(outgoing, "exp", split_axis=0, concat_axis=0, tiled=True)
    slot_rows = arrived.reshape(n_exp * capacity, width)
    gate_proj = jnp.dot(slot_rows, w_gate[0], preferred_element_type=jnp.float32)
    up_proj = jnp.dot(slot_rows, w_up[0], preferred_element_type=jnp.float32)
    hidden = (jax.nn.silu(gate_proj) * up_proj).astype(jnp.bfloat16)
    weight_tok = jnp.sum(gates[:, :, None] * chosen.astype(jnp.float32), axis=1)
    combine_table = weight_tok[:, :, None] * placed.astype(jnp.float32)
    combine_table = jnp.broadcast_to(
        combine_table[:, :, None, :], (block_rows, expert_count, group_size, capacity)
    )
    combine_table = combine_table.reshape(block_rows, n_exp * capacity)
    down_local = w_down[0]
    feature_sums = lax.psum_scatter(
        lax.dot_general(
            down_local, hidden, (((0,), (1,)), ((), ())), preferred_element_type=jnp.float32
        ).astype(jnp.bfloat16),
        "tp",
        scatter_dimension=0,
        tiled=True,
    ).astype(jnp.float32)
    returned = lax.all_to_all(
        feature_sums.reshape(share, n_exp, capacity).astype(jnp.bfloat16),
        "exp",
        split_axis=1,
        concat_axis=1,
        tiled=True,
    ).astype(jnp.float32)
    mixed_cols = lax.dot_general(
        returned.reshape(share, n_exp * capacity),
        combine_table,
        (((1,), (1,)), ((), ())),
        precision=lax.Precision.HIGHEST,
        preferred_element_type=jnp.float32,
    )
    owned = lax.all_to_all(
        mixed_cols.astype(jnp.bfloat16), "tp", split_axis=1, concat_axis=0, tiled=True
    )
    return owned.T


def solution(mesh):
    return jax.shard_map(
        local,
        mesh=mesh,
        in_specs=(
            P(("dp", "exp", "tp"), None),
            P(("dp", "exp"), None),
            P(("dp", "exp"), None),
            P("exp", None, "tp"),
            P("exp", None, "tp"),
            P("exp", "tp", None),
        ),
        out_specs=P(("dp", "exp", "tp"), None),
        check_vma=False,
    )
```

profile of v0, /device:TPU:1, one launch (start us, length us, event | category | flops | bytes accessed | tf_op | source)
XLA Modules:
  0.0 250.5 jit_solution(6891052318980123817)
XLA Ops:
  6.5 0.0 copy-start
  6.5 0.0 reduce-scatter.4.cloned.1.call-start
  6.5 0.8 convert_reduce_fusion
  7.3 0.1 copy.27
  7.5 0.2 reduce_window_sum.11
  7.6 0.1 copy.29
  7.7 0.1 eq.47
  7.8 23.8 %all_gather.3 = bf16[128,3072]{1,0:T(8,128)(2,1)S(1)} all-gather(bf16[8,3072]{1,0:T(8,128)(2,1)} %param.6), channel_id=1, replica_groups=mesh['exp'=8,'tp'=16,'dp'=4] {'tp'}, dimensions={0}, use_global_device_ids=true | all-gather | bytes 835584 | tf_op jit(solution)/shard_map/all_gather | solution.py:16
  31.6 0.1 fusion.20
  31.8 0.7 convolution_convert_fusion.1
  32.4 0.5 broadcast_in_dim.7
  32.9 0.0 copy-start.4
  32.9 98.4 %all_to_all.29 = bf16[8,80,3072]{2,1,0:T(8,128)(2,1)S(1)} all-to-all(bf16[8,80,3072]{2,1,0:T(8,128)(2,1)S(1)} %bitcast.43), channel_id=1, replica_groups=mesh['exp'=8,'tp'=16,'dp'=4] {'exp'}, dimensions={0} | all-to-all | bytes 7864320 | tf_op jit(solution)/shard_map/all_to_all | solution.py:35
  131.3 0.0 copy-start.1
  131.3 1.9 copy-done.1
  133.2 0.0 copy-done.4
  133.2 2.1 fusion.4
  135.3 0.0 copy-done
  135.3 0.0 copy-done.5
  135.3 8.3 %fusion = bf16[3072,640]{0,1:T(8,128)(2,1)} fusion(bf16[1,256,3072]{2,1,0:T(8,128)(2,1)S(1)} %copy-done, bf16[640,3072]{1,0:T(8,128)(2,1)} %bitcast.46, bf16[1,3072,256]{2,1,0:T(8,128)(2,1)S(1)} %copy-done.5, f32[640,256]{1,0:T(8,128)} %fusion.4), kind=kOutput, calls=%fused_computation.1 | convolution fusion | flops 2016215040 | bytes 11665408 | tf_op jit(solution)/shard_map/dot_general | solution.py:48
  143.6 6.0 %copy.32 = bf16[3072,640]{1,0:T(8,128)(2,1)} copy(bf16[3072,640]{0,1:T(8,128)(2,1)} %fusion) | data formatting | bytes 7864320
  149.7 0.0 reduce-scatter.4.cloned.1.call-update
  149.7 56.0 %reduce-scatter.4.cloned.1.call-done = bf16[192,640]{1,0:T(8,128)(2,1)} async-done(((bf16[3072,640]{1,0:T(8,128)(2,1)}), bf16[192,640]{1,0:T(8,128)(2,1)}) %reduce-scatter.4.cloned.1.call-update) | async-done | bytes 245776
  205.7 1.8 copy.33
  207.5 6.1 %all-to-all-start.1 = ((bf16[192,8,80]{0,2,1:T(8,128)(2,1)}), bf16[192,8,80]{0,2,1:T(8,128)(2,1)S(1)}, u32[]{:S(2)}, u32[]{:S(2)}) async-start(bf16[192,8,80]{0,2,1:T(8,128)(2,1)} %bitcast.9), calls=%async_computation.1 | async-start | bytes 655360 | tf_op jit(solution)/shard_map/all_to_all | solution.py:55
  213.6 0.0 copy-done.2
  213.6 0.0 copy-done.3
  213.6 10.1 %all-to-all-done.1 = bf16[192,8,80]{0,2,1:T(8,128)(2,1)S(1)} async-done(((bf16[192,8,80]{0,2,1:T(8,128)(2,1)}), bf16[192,8,80]{0,2,1:T(8,128)(2,1)S(1)}, u32[]{:S(2)}, u32[]{:S(2)}) %all-to-all-start.1) | async-done | bytes 245792 | tf_op jit(solution)/shard_map/all_to_all | solution.py:55
  223.7 0.5 convolution_convert_fusion.2
  224.2 0.1 copy.30
  224.3 18.6 %all_to_all.30 = bf16[192,16,8]{0,2,1:T(8,128)(2,1)S(1)} all-to-all(bf16[192,16,8]{0,2,1:T(8,128)(2,1)S(1)} %bitcast.49), channel_id=1, replica_groups=mesh['exp'=8,'tp'=16,'dp'=4] {'tp'}, dimensions={1} | all-to-all | bytes 98304 | tf_op jit(solution)/shard_map/all_to_all | solution.py:69
  243.0 0.7 all_to_all.25
  (9 shorter events, 0.1 us)
Async XLA Ops:
  6.5 128.7 %copy-start = (bf16[1,256,3072]{2,1,0:T(8,128)(2,1)S(1)}, bf16[1,256,3072]{2,1,0:T(8,128)(2,1)}, u32[]{:S(2)}) copy-start(bf16[1,256,3072]{2,1,0:T(8,128)(2,1)} %param.11) | copy-start | bytes 4718596
  6.5 199.1 %reduce-scatter.4.cloned.1.call-start = ((), (), s32[]{:S(2)}) async-start(), calls=%async_computation.4 | async-start | bytes 4177920
  32.9 100.3 %copy-start.4 = (bf16[1,3072,256]{2,1,0:T(8,128)(2,1)S(1)}, bf16[1,3072,256]{2,1,0:T(8,128)(2,1)}, u32[]{:S(2)}) copy-start(bf16[1,3072,256]{2,1,0:T(8,128)(2,1)} %param.9) | copy-start | bytes 4718596
  131.3 1.9 copy-start.1
  133.2 2.1 copy-start.5
  149.6 63.9 %copy-start.2 = (s32[128,2]{0,1:T(2,128)S(1)}, s32[128,2]{0,1:T(2,128)}, u32[]{:S(2)}) copy-start(s32[128,2]{0,1:T(2,128)} %param.7) | copy-start | bytes 3076
  149.6 63.9 %copy-start.3 = (f32[128,2]{0,1:T(2,128)S(1)}, f32[128,2]{0,1:T(2,128)}, u32[]{:S(2)}) copy-start(f32[128,2]{0,1:T(2,128)} %param.8) | copy-start | bytes 3076
  207.5 16.2 %all-to-all-start.1 = ((bf16[192,8,80]{0,2,1:T(8,128)(2,1)}), bf16[192,8,80]{0,2,1:T(8,128)(2,1)S(1)}, u32[]{:S(2)}, u32[]{:S(2)}) async-start(bf16[192,8,80]{0,2,1:T(8,128)(2,1)} %bitcast.9), calls=%async_computation.1 | async-start | bytes 655360 | tf_op jit(solution)/shard_map/all_to_all | solution.py:55
Sparse Core Ops, SparseCore 0:
  149.8 55.8 reduce-scatter.3
where the time goes:
time: 251 us
  blocking collectives  141 us (56%)
  waiting for transfers between devices  66.1 us (26%)
  between operations  13.5 us (5%)
  matrix products  11.5 us (5%)
  local copies, waits for them, and re-layouts  11.4 us (5%)
  starting transfers between devices  6.09 us (2%)
    all_to_all x1, blocking collectives, local(): lax.all_to_all(outgoing, 'exp', split_axis=0, concat_axis=0, tiled=True)  98.4 us
    unnamed x2, waiting for transfers between devices  56 us
    all_gather x1, blocking collectives, local(): gathered = lax.all_gather(tokens, 'tp', axis=0, tiled=True)  23.8 us
    all_to_all x1, blocking collectives, local(): lax.all_to_all(mixed_cols.astype(jnp.bfloat16), 'tp', split_axis=1, conca...  18.6 us
    all_to_all x1, waiting for transfers between devices, local(): lax.all_to_all(feature_sums.reshape(share, n_exp, capacity).astype(jnp.bf...  10.1 us
    unnamed x14, local copies, waits for them, and re-layouts  9.79 us
    dot_general x1, matrix products, local(): lax.dot_general(down_local, hidden, (((0,), (1,)), ((), ())), preferred_e...  8.32 us
    all_to_all x1, starting transfers between devices, local(): lax.all_to_all(feature_sums.reshape(share, n_exp, capacity).astype(jnp.bf...  6.09 us
  transfers between devices with their start and end apart: 2, of which 2 were waited for; matrix products, arithmetic and copies ran while one was open for 0% of the time, Pallas kernels for 0%

commit v1 on v0

v1 whole, which is shorter than its diff:
```python
import functools

import jax
import jax.numpy as jnp
from jax import lax
from jax.experimental import pallas as pl
from jax.experimental.pallas import tpu as pltpu
from jax.sharding import PartitionSpec as P

MESH = pl.DeviceIdType.MESH
EXPERTS = 4
NZ = 8
NY = 8
NC = 2
ROWS = 128
CAP = 80
BLOCKS = NZ // NC
OFFSETS = ((0, 2, 6, 4), (1, 7, 3, 5))
STEPS = tuple((3, 4) if j % 2 == 0 else (4, 3) for j in range(BLOCKS))


def schedule():
    tasks = []
    for j in range(BLOCKS):
        start = 5.0 * j
        for h in range(1, 6):
            tasks.append((start + 2.7 * (h - 1), 0, "gather", j, h))
        full = start + 2.7 * 4
        tasks.append((full + 0.1, 1, "up", j, 0))
        tasks.append((full + 1.5, 2, "down", j, 0))
        for s in range(1, 6):
            tasks.append((full + 2.3 + 3.4 * (s - 1), 3, "scatter", j, s))
    tasks.sort()
    return [(kind, j, h) for _, _, kind, j, h in tasks]


def kernel(
    tok, routes_in, gates_in, wg, wu, wd, out,
    routes, gates, arrived, gate_w, up_w, down_w, hot, back_hot, weight, packed, rows, hidden, partial,
    leaving, coming, summed, returned, mixed, owned,
    p1s, p1r, lw, ws, wr, p3s, p3r, ags, agr, rss, rsr, rts, rtr, fs, fr,
):
    z = lax.axis_index("exp")
    t = lax.axis_index("tp")
    y = t // NC
    c = lax.rem(t, NC)
    home_core = lax.rem(z, NC)
    parity = lax.rem(z + c, NC)
    is_home = parity == 0
    share = rows.shape[-1]
    width = tok.shape[-1]

    def at(zz, yy, cc):
        return {"exp": zz, "tp": yy * NC + cc}

    def ring(v, n):
        return lax.rem(v + n, n)

    def send(src, dst, ssem, rsem, device):
        copy = pltpu.make_async_remote_copy(
            src_ref=src, dst_ref=dst, send_sem=ssem, recv_sem=rsem, device_id=device, device_id_type=MESH
        )
        copy.start()

    def sent(src, sem):
        pltpu.make_async_copy(src, src, sem).wait()

    def came(dst, sem):
        pltpu.make_async_copy(dst, dst, sem).wait()

    def chunk(ref, index):
        return ref.at[:, pl.ds(pl.multiple_of(index * share, 128), share)]

    weights = ((wg, gate_w), (wu, up_w), (wd, down_w))
    for i, (src, dst) in enumerate(weights):
        pltpu.make_async_copy(src.at[0], dst.at[c], lw.at[i]).start()

    routing = ((routes_in, routes), (gates_in, gates))
    for i, (src, dst) in enumerate(routing):
        pltpu.make_async_copy(src, dst, lw.at[3 + i]).start()

    barrier = pltpu.get_barrier_semaphore()
    for dy in range(NY):
        for dc in range(NC):
            if dy or dc:
                pl.semaphore_signal(
                    barrier, inc=1, device_id=at(z, ring(y + dy, NY), ring(c + dc, NC)), device_id_type=MESH
                )
    for dz in range(1, NZ):
        pl.semaphore_signal(barrier, inc=1, device_id=at(ring(z + dz, NZ), y, c), device_id_type=MESH)
    pl.semaphore_wait(barrier, NY * NC - 1 + NZ - 1)

    for dy in (4, 3, 5, 2, 6, 1, 7):
        to = ring(y + dy, NY)
        send(chunk(tok, to), arrived.at[t], p1s.at[dy], p1r.at[t], at(z, to, home_core))

    @pl.when(is_home)
    def _():
        pltpu.make_async_copy(chunk(tok, y), arrived.at[t], p1r.at[t]).start()

    @pl.when(jnp.logical_not(is_home))
    def _():
        send(chunk(tok, y), arrived.at[t], p1s.at[0], p1r.at[t], at(z, y, home_core))

    for i, (src, dst) in enumerate(weights):
        send(src.at[0], dst.at[c], ws.at[i], wr.at[i], at(z, y, 1 - c))

    for i, (src, dst) in enumerate(routing):
        came(dst, lw.at[3 + i])

    def pick(e, first, second):
        here = [jnp.broadcast_to(routes[k:k + 1, :], (ROWS, ROWS)) == e for k in range(2)]
        return jnp.where(here[0], first, 0.0) + jnp.where(here[1], second, 0.0)

    @pl.when(is_home)
    def _():
        row_ids = lax.broadcasted_iota(jnp.int32, (ROWS, ROWS), 0)
        col_ids = lax.broadcasted_iota(jnp.int32, (ROWS, ROWS), 1)
        earlier = jnp.where(row_ids < col_ids, 1.0, 0.0).astype(jnp.bfloat16)
        slots = row_ids.astype(jnp.float32)
        g0, g1 = (jnp.broadcast_to(gates[k:k + 1, :], (ROWS, ROWS)) for k in range(2))
        for e in range(EXPERTS):
            mine = pick(e, 1.0, 1.0)
            before = jnp.dot(mine.astype(jnp.bfloat16), earlier, preferred_element_type=jnp.float32)
            placed = jnp.where(before == slots, mine, 0.0)
            hot[e] = placed.astype(jnp.bfloat16)
            back_hot[e] = placed.T.astype(jnp.bfloat16)
            gate = jnp.sum(jnp.where(row_ids == col_ids, pick(e, g0, g1), 0.0), axis=1, keepdims=True)
            weight[e] = jnp.broadcast_to(gate, (ROWS, 128))
        for i in range(NY * NC):
            came(arrived.at[i], p1r.at[i])
        block = arrived[...].astype(jnp.float32).reshape(ROWS, share).astype(jnp.bfloat16)
        for e in range(EXPERTS):
            packed[e] = jnp.dot(hot[e, :CAP, :], block, preferred_element_type=jnp.float32).astype(jnp.bfloat16)
        for j in range(BLOCKS):
            for side in range(2):
                d = (NZ - OFFSETS[side][j]) % NZ
                to = ring(z + d, NZ)
                src = packed.at[to // (NZ // EXPERTS)]
                if d == 0:
                    pltpu.make_async_copy(src, rows.at[j, y], p3r.at[j]).start()
                else:
                    send(src, rows.at[j, y], p3s.at[d], p3r.at[j], at(to, y, c))

    def gather(j, h):
        if h == 1:
            came(rows.at[j, y], p3r.at[j])
        for way, sign in ((0, 1), (1, -1)):
            count = STEPS[j][way]
            if 2 <= h <= count + 1:
                came(rows.at[j, ring(y - sign * (h - 1), NY)], agr.at[j, way, h - 2])
            if h <= count:
                piece = rows.at[j, ring(y - sign * (h - 1), NY)]
                send(piece, piece, ags.at[j, way, h - 1], agr.at[j, way, h - 1], at(z, ring(y + sign, NY), c))

    def up(j):
        if j == 0:
            for i, (src, dst) in enumerate(weights[:2]):
                came(dst.at[c], lw.at[i])
                came(dst.at[1 - c], wr.at[i])
        x = jnp.concatenate([rows[j, f] for f in range(NY)], axis=1)
        for core in range(NC):
            g = jnp.dot(x, gate_w[core], preferred_element_type=jnp.float32)
            u = jnp.dot(x, up_w[core], preferred_element_type=jnp.float32)
            n = g.shape[1]
            hidden[j, :, core * n:(core + 1) * n] = (g / (1.0 + jnp.exp(-g)) * u).astype(jnp.bfloat16)

    def down(j):
        if j == 0:
            came(down_w.at[c], lw.at[2])
            came(down_w.at[1 - c], wr.at[2])
        n = down_w.shape[1]
        for f in range(0, NY, 2):
            lo, hi = f * share, (f + 2) * share
            r = jnp.dot(hidden[j, :, :n], down_w[0, :, lo:hi], preferred_element_type=jnp.float32)
            r += jnp.dot(hidden[j, :, n:], down_w[1, :, lo:hi], preferred_element_type=jnp.float32)
            partial[j, f] = r[:, :share]
            partial[j, f + 1] = r[:, share:]

    def scatter(j, s):
        for way, sign in ((0, 1), (1, -1)):
            count = STEPS[j][way]
            if s > count:
                continue
            piece = partial[j, ring(y + sign * (count - s + 1), NY)]
            if s >= 2:
                came(coming.at[j, way, s - 2], rsr.at[j, way, s - 2])
                piece = piece + coming[j, way, s - 2].astype(jnp.float32)
            leaving[j, way, s - 1] = piece.astype(jnp.bfloat16)
            send(
                leaving.at[j, way, s - 1], coming.at[j, way, s - 1], rss.at[j, way, s - 1], rsr.at[j, way, s - 1],
                at(z, ring(y + sign, NY), c),
            )
        if s == 5:
            total = partial[j, y]
            for way in range(2):
                last = STEPS[j][way] - 1
                came(coming.at[j, way, last], rsr.at[j, way, last])
                total = total + coming[j, way, last].astype(jnp.float32)
            summed[j] = total.astype(jnp.bfloat16)
            back = ring(z + OFFSETS[0][j] + parity * (OFFSETS[1][j] - OFFSETS[0][j]), NZ)
            if j == 0:
                @pl.when(is_home)
                def _():
                    pltpu.make_async_copy(summed.at[j], returned.at[z], rtr.at[z]).start()

                @pl.when(jnp.logical_not(is_home))
                def _():
                    send(summed.at[j], returned.at[z], rts.at[j], rtr.at[z], at(back, y, c))
            else:
                send(summed.at[j], returned.at[z], rts.at[j], rtr.at[z], at(back, y, c))

    for kind, j, h in schedule():
        if kind == "gather":
            gather(j, h)
        elif kind == "up":
            up(j)
        elif kind == "down":
            down(j)
        else:
            scatter(j, h)

    @pl.when(is_home)
    def _():
        for i in range(NZ):
            came(returned.at[i], rtr.at[i])
        total = jnp.zeros((ROWS, share), jnp.float32)
        for e in range(EXPERTS):
            picked = jnp.zeros((ROWS, share), jnp.float32)
            for g in range(NZ // EXPERTS):
                picked += jnp.dot(
                    back_hot[e, :, :CAP], returned[e * (NZ // EXPERTS) + g], preferred_element_type=jnp.float32
                )
            total += jnp.concatenate([weight[e]] * (share // 128), axis=1) * picked
        mixed[...] = total.reshape(NY * NC, ROWS // (NY * NC), share).astype(jnp.bfloat16)
        for dy in (4, 3, 5, 2, 6, 1, 7, 0):
            for dc in range(NC):
                to, core = ring(y + dy, NY), ring(c + dc, NC)
                src = mixed.at[to * NC + core]
                if dy == 0 and dc == 0:
                    pltpu.make_async_copy(src, chunk(owned, y), fr.at[y]).start()
                else:
                    send(src, chunk(owned, y), fs.at[dy * NC + dc], fr.at[y], at(z, to, core))

    for i in range(NY):
        came(owned.at[:, i * share:(i + 1) * share], fr.at[i])
    out[...] = owned[...]

    for dy in range(1, NY):
        sent(chunk(tok, y), p1s.at[dy])
    for i, (src, dst) in enumerate(weights):
        sent(src.at[0], ws.at[i])
    for j in range(BLOCKS):
        for way in range(2):
            for h in range(STEPS[j][way]):
                sent(rows.at[j, 0], ags.at[j, way, h])
                sent(leaving.at[j, way, h], rss.at[j, way, h])
        if j > 0:
            sent(summed.at[j], rts.at[j])

    @pl.when(is_home)
    def _():
        for d in range(1, NZ):
            sent(packed.at[0], p3s.at[d])
        for i in range(1, NY * NC):
            sent(mixed.at[0], fs.at[i])

    @pl.when(jnp.logical_not(is_home))
    def _():
        sent(chunk(tok, y), p1s.at[0])
        sent(summed.at[0], rts.at[0])


def local(tokens, routes, gates, w_gate, w_up, w_down):
    tok_dev, width = tokens.shape
    hid = w_gate.shape[2]
    share = width // NY
    bf16, f32 = jnp.bfloat16, jnp.float32
    vmem = pl.BlockSpec(memory_space=pltpu.VMEM)
    hbm = pl.BlockSpec(memory_space=pltpu.HBM)
    dma = pltpu.SemaphoreType.DMA
    return pl.pallas_call(
        kernel,
        out_shape=jax.ShapeDtypeStruct((tok_dev, width), bf16),
        in_specs=[hbm] * 6,
        out_specs=vmem,
        scratch_shapes=[
            pltpu.VMEM((2, ROWS), jnp.int32),
            pltpu.VMEM((2, ROWS), f32),
            pltpu.VMEM((NY * NC, tok_dev, share), bf16),
            pltpu.VMEM((NC, width, hid), bf16),
            pltpu.VMEM((NC, width, hid), bf16),
            pltpu.VMEM((NC, hid, width), bf16),
            pltpu.VMEM((EXPERTS, ROWS, ROWS), bf16),
            pltpu.VMEM((EXPERTS, ROWS, ROWS), bf16),
            pltpu.VMEM((EXPERTS, ROWS, 128), f32),
            pltpu.VMEM((EXPERTS, CAP, share), bf16),
            pltpu.VMEM((BLOCKS, NY, CAP, share), bf16),
            pltpu.VMEM((BLOCKS, CAP, NC * hid), bf16),
            pltpu.VMEM((BLOCKS, NY, CAP, share), f32),
            pltpu.VMEM((BLOCKS, 2, 4, CAP, share), bf16),
            pltpu.VMEM((BLOCKS, 2, 4, CAP, share), bf16),
            pltpu.VMEM((BLOCKS, CAP, share), bf16),
            pltpu.VMEM((NZ, CAP, share), bf16),
            pltpu.VMEM((NY * NC, tok_dev, share), bf16),
            pltpu.VMEM((tok_dev, width), bf16),
            dma((NY,)), dma((NY * NC,)),
            dma((5,)), dma((3,)), dma((3,)),
            dma((NZ,)), dma((BLOCKS,)),
            dma((BLOCKS, 2, 4)), dma((BLOCKS, 2, 4)),
            dma((BLOCKS, 2, 4)), dma((BLOCKS, 2, 4)),
            dma((BLOCKS,)), dma((NZ,)),
            dma((NY * NC,)), dma((NY,)),
        ],
        compiler_params=pltpu.CompilerParams(
            collective_id=0, has_side_effects=True, vmem_limit_bytes=62 * 2**20
        ),
        name="moe",
    )(tokens, routes.T, gates.T, w_gate, w_up, w_down)


def solution(mesh):
    return jax.shard_map(
        local,
        mesh=mesh,
        in_specs=(
            P(("dp", "exp", "tp"), None),
            P(("dp", "exp"), None),
            P(("dp", "exp"), None),
            P("exp", None, "tp"),
            P("exp", None, "tp"),
            P("exp", "tp", None),
        ),
        out_specs=P(("dp", "exp", "tp"), None),
        check_vma=False,
    )
```

time: 251 us -> 90 us (0.36)
  blocking collectives: 141 us -> 0 us
  Pallas kernels: 0 us -> 88.4 us
  waiting for transfers between devices: 66.1 us -> 0 us
  between operations: 13.5 us -> 0.01 us
  matrix products: 11.5 us -> 0 us
  local copies, waits for them, and re-layouts: 11.4 us -> 1.42 us
  starting transfers between devices: 6.09 us -> 0 us
    all_to_all x2 -> x0, blocking collectives: 117 us -> none  [the longest x1 98.4 us: local(): lax.all_to_all(outgoing, 'exp', split_axis=0, concat_axis=0, tiled=True)]
    pallas_call x0 -> x1, Pallas kernels: none -> 88.4 us  [local(): pl.pallas_call(kernel, out_shape=jax.ShapeDtypeStruct((tok_dev, width), b...]
    unnamed x2 -> x0, waiting for transfers between devices: 56 us -> none
    all_gather x1 -> x0, blocking collectives: 23.8 us -> none  [local(): gathered = lax.all_gather(tokens, 'tp', axis=0, tiled=True)]
    dot_general x4 -> x0, matrix products: 11.5 us -> none  [the longest x1 8.32 us: local(): lax.dot_general(down_local, hidden, (((0,), (1,)), ((), ())), preferred_e...]
    all_to_all x1 -> x0, waiting for transfers between devices: 10.1 us -> none  [local(): lax.all_to_all(feature_sums.reshape(share, n_exp, capacity).astype(jnp.bf...]
    unnamed x14 -> x1, local copies, waits for them, and re-layouts: 9.79 us -> 1.42 us
    all_to_all x1 -> x0, starting transfers between devices: 6.09 us -> none  [local(): lax.all_to_all(feature_sums.reshape(share, n_exp, capacity).astype(jnp.bf...]
  transfers between devices with their start and end apart: 2 -> 0, of which waited for: 2 -> 0; matrix products, arithmetic and copies ran while one was open for 0% -> 0% of each run, Pallas kernels for 0% -> 0%
where the time goes in v1:
time: 90 us; the launch traced here: 89.8 us
  Pallas kernels  88.4 us (98%)
  local copies, waits for them, and re-layouts  1.42 us (2%)
    pallas_call x1, Pallas kernels, local(): pl.pallas_call(kernel, out_shape=jax.ShapeDtypeStruct((tok_dev, width), b...  88.4 us

profile of v1, /device:TPU:1, one launch (start us, length us, event | category | flops | bytes accessed | tf_op | source)
XLA Modules:
  0.0 89.8 jit_solution(566635040311661164)
XLA Ops:
  0.0 88.4 %moe.1 = bf16[8,3072]{1,0:T(8,128)(2,1)} custom-call(bf16[8,3072]{1,0:T(8,128)(2,1)} %tok.1, s32[2,128]{1,0:T(2,128)} %bitcast.2, f32[2,128]{1,0:T(2,128)} %bitcast.3, bf16[1,3072,256]{2,1,0:T(8,128)(2,1)} %wg.1, bf16[1,3072,256]{2,1,0:T(8,128)(2,1)} %wu.1, bf16[1,256,3072]{2,1,0:T(8,128)(2,1)} %wd.1), custom_call_target="tpu_custom_call" | custom-call | tf_op jit(solution)/shard_map/moe/pallas_call | solution.py:282
  88.4 1.4 %copy.8 = bf16[8,3072]{1,0:T(8,128)(2,1)} copy(bf16[8,3072]{1,0:T(8,128)(2,1)} %moe.1) | data formatting | bytes 98304

commit v2 on v1

v2 whole, which is shorter than its diff:
```python
import jax
import jax.numpy as jnp
from jax import lax
from jax.experimental import pallas as pl
from jax.experimental.pallas import tpu as pltpu
from jax.sharding import PartitionSpec as P

MESH = pl.DeviceIdType.MESH
EXPERTS = 4
NZ = 8
NY = 8
NC = 2
ROWS = 128
CAP = 80
BLOCKS = NZ // NC
OFFSETS = ((0, 2, -2, 4), (1, 3, -1, -3))


GROUPS = ((0, 2), (1, 3))
GATHER = (((0, 1, 2, 3), (0,)), ((0, 0, 2, 3), (0,)), ((0,), (0, 1, 2, 3)), ((0,), (0, 0, 2, 3)))
SCATTER = (((0, 1, 2, 3), (0,)), ((0, 0, 2, 3), (0,)), ((0,), (0, 1, 2, 3)), ((0,), (0, 0, 2, 3)))
ORDER = (
    ("ag", 0, 0, 1),
    ("ag", 0, 1, 1),
    ("zo", 0),
    ("zo", 1),
    ("ag", 1, 1, 1),
    ("ag", 0, 0, 2),
    ("ag", 2, 1, 1),
    ("ag", 1, 0, 2),
    ("ag", 3, 1, 2),
    ("zf", 1, (0, 2)),
    ("ag", 1, 0, 3),
    ("ag", 2, 1, 2),
    ("ag", 1, 0, 1),
    ("zf", 0, (0, 2)),
    ("ag", 3, 1, 3),
    ("ag", 0, 0, 3),
    ("zf", 3, (1, 2)),
    ("ag", 2, 1, 3),
    ("zf", 1, (0, 3)),
    ("ag", 3, 1, 1),
    ("ag", 1, 0, 4),
    ("zf", 3, (1, 3)),
    ("ag", 3, 0, 1),
    ("ag", 3, 1, 4),
    ("ag", 2, 1, 4),
    ("zf", 0, (0, 3)),
    ("zf", 2, (1, 2)),
    ("zf", 2, (1, 3)),
    ("ag", 0, 0, 4),
    ("ag", 2, 0, 1),
    ("up", 1, 0),
    ("up", 1, 1),
    ("down", 1, 0),
    ("down", 1, 1),
    ("zs", 3, (0, 3)),
    ("rs", 3, 1, 4),
    ("rs", 1, 0, 4),
    ("zs", 1, (1, 3)),
    ("rs", 3, 0, 1),
    ("zs", 3, (0, 2)),
    ("rs", 1, 1, 1),
    ("up", 0, 0),
    ("up", 0, 1),
    ("down", 0, 0),
    ("down", 0, 1),
    ("rs", 2, 1, 4),
    ("zs", 0, (1, 3)),
    ("rs", 0, 0, 4),
    ("zs", 2, (0, 3)),
    ("rs", 0, 1, 1),
    ("rs", 1, 0, 1),
    ("rs", 1, 0, 3),
    ("zs", 0, (1, 2)),
    ("rs", 3, 1, 3),
    ("zs", 1, (1, 2)),
    ("rs", 2, 1, 3),
    ("rs", 0, 0, 3),
    ("zs", 2, (0, 2)),
    ("rs", 1, 0, 2),
    ("rs", 3, 1, 1),
    ("rs", 2, 1, 2),
    ("rs", 3, 1, 2),
    ("rs", 0, 0, 2),
    ("fin", 1),
    ("rs", 2, 0, 1),
    ("rs", 2, 1, 1),
    ("rs", 0, 0, 1),
    ("fin", 3),
    ("fin", 2),
    ("fin", 0),
)


def missing(mine, other):
    if sum(map(len, mine)) == NY - 1:
        return []
    return [
        (w, d) for w in range(2) for d in range(len(mine[w]) + 1, len(other[w]) + 1)
        if not (d == NY // 2 and len(mine[1 - w]) == d)
    ]


def kernel(
    tok_in, routes_in, gates_in, wg, wu, wd, out,
    tok, routes, gates, arrived, gate_w, up_w, down_w, hot, back_hot, weight, packed, rows, hidden, partial,
    leaving, coming, leaving_z, coming_z, summed, returned, mixed, owned,
    p1s, p1r, lw, ws, wr, p3s, p3r, zos, ags, agr, zfs, zfr, rss, rsr, zss, zsr, rts, rtr, fs, fr,
):
    groups, ag, rs, order = GROUPS, GATHER, SCATTER, ORDER
    z = lax.axis_index("exp")
    t = lax.axis_index("tp")
    y = t // NC
    c = lax.rem(t, NC)
    home_core = lax.rem(z, NC)
    side = lax.rem(z + c, NC)
    is_home = side == 0
    turn = 2 * home_core - 1
    share = rows.shape[-1]

    def at(zz, yy, cc):
        return {"exp": zz, "tp": yy * NC + cc}

    def ring(v, n):
        return lax.rem(v + n, n)

    def send(src, dst, ssem, rsem, device):
        pltpu.make_async_remote_copy(
            src_ref=src, dst_ref=dst, send_sem=ssem, recv_sem=rsem, device_id=device, device_id_type=MESH
        ).start()

    def wait(ref, sem):
        pltpu.make_async_copy(ref, ref, sem).wait()

    def chunk(ref, index):
        return ref.at[:, pl.ds(pl.multiple_of(index * share, 128), share)]

    partner = z - turn
    weights = ((wg, gate_w), (wu, up_w), (wd, down_w))
    small = ((tok_in, tok), (routes_in, routes), (gates_in, gates))
    for i, (src, dst) in enumerate(small):
        pltpu.make_async_copy(src, dst, lw.at[3 + i]).start()
    barrier = pltpu.get_barrier_semaphore()
    for dy in (4, 3, 5, 2, 6, 1, 7, 0):
        for dc in range(NC):
            if dy or dc:
                pl.semaphore_signal(
                    barrier, inc=1, device_id=at(z, ring(y + dy, NY), ring(c + dc, NC)), device_id_type=MESH
                )
    for dz in (4, 3, 5, 2, 6, 1, 7):
        pl.semaphore_signal(barrier, inc=1, device_id=at(ring(z + dz, NZ), y, c), device_id_type=MESH)
    for i, (src, dst) in enumerate(weights):
        pltpu.make_async_copy(src.at[0], dst.at[c], lw.at[i]).start()
    wait(tok, lw.at[3])
    pl.semaphore_wait(barrier, NY * NC - 1 + NZ - 1)

    for dy in (4, 3, 5, 2, 6, 1, 7):
        to = ring(y + dy, NY)
        send(chunk(tok, to), arrived.at[t], p1s.at[dy], p1r.at[t], at(z, to, home_core))

    @pl.when(is_home)
    def _():
        pltpu.make_async_copy(chunk(tok, y), arrived.at[t], p1r.at[t]).start()

    @pl.when(jnp.logical_not(is_home))
    def _():
        send(chunk(tok, y), arrived.at[t], p1s.at[0], p1r.at[t], at(z, y, home_core))

    for i, (src, dst) in enumerate(weights):
        send(src.at[0], dst.at[c], ws.at[i], wr.at[i], at(z, y, 1 - c))

    for i, (src, dst) in enumerate(small[1:]):
        wait(dst, lw.at[4 + i])

    def pick(e, first, second):
        here = [jnp.broadcast_to(routes[k:k + 1, :], (ROWS, ROWS)) == e for k in range(2)]
        return jnp.where(here[0], first, 0.0) + jnp.where(here[1], second, 0.0)

    @pl.when(is_home)
    def _():
        row_ids = lax.broadcasted_iota(jnp.int32, (ROWS, ROWS), 0)
        col_ids = lax.broadcasted_iota(jnp.int32, (ROWS, ROWS), 1)
        earlier = jnp.where(row_ids < col_ids, 1.0, 0.0).astype(jnp.bfloat16)
        slots = row_ids.astype(jnp.float32)
        for e in range(EXPERTS):
            mine = pick(e, 1.0, 1.0)
            before = jnp.dot(mine.astype(jnp.bfloat16), earlier, preferred_element_type=jnp.float32)
            placed = jnp.where(before == slots, mine, 0.0)
            hot[e] = placed.astype(jnp.bfloat16)
        for i in range(NY * NC):
            wait(arrived.at[i], p1r.at[i])
        block = arrived[...].astype(jnp.float32).reshape(ROWS, share).astype(jnp.bfloat16)
        for j, k in ((0, 0), (1, 1), (1, 0), (0, 1)):
            to = ring(z - turn * OFFSETS[0][j], NZ) if k == 0 else ring(z + turn * OFFSETS[1][j], NZ)
            e = to // (NZ // EXPERTS)
            packed[2 * k + j] = jnp.dot(hot[e, :CAP, :], block, preferred_element_type=jnp.float32).astype(jnp.bfloat16)
            if k == 0 and j == 0:
                pltpu.make_async_copy(packed.at[0], rows.at[j, y], p3r.at[j]).start()
            else:
                send(packed.at[2 * k + j], rows.at[j, y], p3s.at[2 * k + j], p3r.at[j], at(to, y, c))

    waited = set()

    def need(kind, j, *where):
        key = (kind, j) + where
        if key in waited:
            return
        waited.add(key)
        if kind == "p3":
            wait(rows.at[j, y], p3r.at[j])
        elif kind == "ag":
            way, h = where
            wait(rows.at[j, ring(y - (1 - 2 * way) * h, NY)], agr.at[j, way, h - 1])
        elif kind == "zf":
            (way, d), i = where
            wait(rows.at[j, ring(y - (1 - 2 * way) * d, NY)], zfr.at[j, i])
        elif kind == "rs":
            way, s = where
            wait(coming.at[j, way, s - 1], rsr.at[j, way, s - 1])
        elif kind == "zs":
            wait(coming_z.at[j, where[0]], zsr.at[j, where[0]])

    def gather(j, way, d):
        sign, parent = 1 - 2 * way, ag[j][way][d - 1]
        piece = rows.at[j, ring(y - sign * parent, NY)]
        need("ag", j, way, parent) if parent else need("p3", j)
        send(
            piece, piece, ags.at[j, way, d - 1], agr.at[j, way, d - 1],
            at(z, ring(y + sign * (d - parent), NY), c),
        )

    def share_own(j):
        need("p3", j)
        send(rows.at[j, y], rows.at[j ^ 2, y], zos.at[j], p3r.at[j ^ 2], at(partner, y, c))

    def forward(j, far):
        other = j ^ 2
        i = missing(ag[other], ag[j]).index(far)
        need("ag", j, *far)
        f = ring(y - (1 - 2 * far[0]) * far[1], NY)
        send(rows.at[j, f], rows.at[other, f], zfs.at[j, i], zfr.at[other, i], at(partner, y, c))

    def up(g, core):
        if core == 0:
            for j in groups[g]:
                need("p3", j)
                for way in range(2):
                    for h in range(1, len(ag[j][way]) + 1):
                        need("ag", j, way, h)
                for i, far in enumerate(missing(ag[j], ag[j ^ 2])):
                    need("zf", j, far, i)
        if "up" not in waited:
            waited.add("up")
            for i, (src, dst) in enumerate(weights[:2]):
                wait(dst.at[c], lw.at[i])
                wait(dst.at[1 - c], wr.at[i])
        x = jnp.concatenate(
            [jnp.concatenate([rows[j, f] for f in range(NY)], axis=1) for j in groups[g]], axis=0
        )
        gp = jnp.dot(x, gate_w[core], preferred_element_type=jnp.float32)
        u = jnp.dot(x, up_w[core], preferred_element_type=jnp.float32)
        n = gp.shape[1]
        hid = (gp / (1.0 + jnp.exp(-gp)) * u).astype(jnp.bfloat16)
        for i, j in enumerate(groups[g]):
            hidden[j, :, core * n:(core + 1) * n] = hid[i * CAP:(i + 1) * CAP]

    def down(g, half):
        if "down" not in waited:
            waited.add("down")
            wait(down_w.at[c], lw.at[2])
            wait(down_w.at[1 - c], wr.at[2])
        n = down_w.shape[1]
        h = jnp.concatenate([hidden[j] for j in groups[g]], axis=0)
        for f in range(half * NY // 2, (half + 1) * NY // 2, 2):
            lo, hi = f * share, (f + 2) * share
            r = jnp.dot(h[:, :n], down_w[0, :, lo:hi], preferred_element_type=jnp.float32)
            r += jnp.dot(h[:, n:], down_w[1, :, lo:hi], preferred_element_type=jnp.float32)
            for i, j in enumerate(groups[g]):
                partial[j, f] = r[i * CAP:(i + 1) * CAP, :share]
                partial[j, f + 1] = r[i * CAP:(i + 1) * CAP, share:]

    def across(j, far):
        other = j ^ 2
        i = missing(rs[j], rs[other]).index(far)
        f = ring(y + (1 - 2 * far[0]) * far[1], NY)
        leaving_z[j, i] = partial[j, f].astype(jnp.bfloat16)
        send(leaving_z.at[j, i], coming_z.at[other, i], zss.at[j, i], zsr.at[other, i], at(partner, y, c))

    def scatter(j, way, d):
        sign, parent = 1 - 2 * way, rs[j][way][d - 1]
        total = partial[j, ring(y + sign * d, NY)]
        far = missing(rs[j ^ 2], rs[j])
        if (way, d) in far:
            i = far.index((way, d))
            need("zs", j, i)
            total = total + coming_z[j, i].astype(jnp.float32)
        total = total + children(j, way, d)
        leaving[j, way, d - 1] = total.astype(jnp.bfloat16)
        send(
            leaving.at[j, way, d - 1], coming.at[j, way, d - 1], rss.at[j, way, d - 1], rsr.at[j, way, d - 1],
            at(z, ring(y + sign * (d - parent), NY), c),
        )

    def children(j, way, d):
        total = 0.0
        for e, parent in enumerate(rs[j][way], 1):
            if parent == d:
                need("rs", j, way, e)
                total = total + coming[j, way, e - 1].astype(jnp.float32)
        return total

    def finish(j):
        total = partial[j, y]
        for way in range(2):
            total = total + children(j, way, 0)
        summed[j] = total.astype(jnp.bfloat16)
        back = ring(z + turn * (OFFSETS[0][j] + side * (OFFSETS[1][j] - OFFSETS[0][j])), NZ)
        if j == 0:
            @pl.when(is_home)
            def _():
                pltpu.make_async_copy(summed.at[j], returned.at[z], rtr.at[z]).start()

            @pl.when(jnp.logical_not(is_home))
            def _():
                send(summed.at[j], returned.at[z], rts.at[j], rtr.at[z], at(back, y, c))
        else:
            send(summed.at[j], returned.at[z], rts.at[j], rtr.at[z], at(back, y, c))

    step = {"ag": gather, "zo": share_own, "zf": forward, "up": up, "down": down, "zs": across, "rs": scatter, "fin": finish}
    for task in order:
        step[task[0]](*task[1:])

    @pl.when(is_home)
    def _():
        diagonal = lax.broadcasted_iota(jnp.int32, (ROWS, ROWS), 0) == lax.broadcasted_iota(jnp.int32, (ROWS, ROWS), 1)
        g0, g1 = (jnp.broadcast_to(gates[k:k + 1, :], (ROWS, ROWS)) for k in range(2))
        for e in range(EXPERTS):
            back_hot[e] = hot[e].astype(jnp.float32).T.astype(jnp.bfloat16)
            gate = jnp.sum(jnp.where(diagonal, pick(e, g0, g1), 0.0), axis=1, keepdims=True)
            weight[e] = jnp.broadcast_to(gate, (ROWS, 128))
        total = jnp.zeros((ROWS, share), jnp.float32)
        for j in [task[1] for task in order if task[0] == "fin"]:
            for k in range(2):
                to = ring(z - turn * OFFSETS[0][j], NZ) if k == 0 else ring(z + turn * OFFSETS[1][j], NZ)
                e = to // (NZ // EXPERTS)
                wait(returned.at[to], rtr.at[to])
                picked = jnp.dot(back_hot[e, :, :CAP], returned[to], preferred_element_type=jnp.float32)
                total += jnp.concatenate([weight[e]] * (share // 128), axis=1) * picked
        mixed[...] = total.reshape(NY * NC, ROWS // (NY * NC), share).astype(jnp.bfloat16)
        for dy in (4, 3, 5, 2, 6, 1, 7, 0):
            for dc in range(NC):
                to, core = ring(y + dy, NY), ring(c + dc, NC)
                src = mixed.at[to * NC + core]
                if dy == 0 and dc == 0:
                    pltpu.make_async_copy(src, chunk(owned, y), fr.at[y]).start()
                else:
                    send(src, chunk(owned, y), fs.at[dy * NC + dc], fr.at[y], at(z, to, core))

    for dy in range(1, NY):
        wait(chunk(tok, y), p1s.at[dy])
    for i, (src, dst) in enumerate(weights):
        wait(src.at[0], ws.at[i])
    for j in range(BLOCKS):
        for way in range(2):
            for h in range(len(ag[j][way])):
                wait(rows.at[j, 0], ags.at[j, way, h])
            for h in range(len(rs[j][way])):
                wait(leaving.at[j, way, h], rss.at[j, way, h])
        for i in range(len(missing(ag[j ^ 2], ag[j]))):
            wait(rows.at[j, 0], zfs.at[j, i])
        for i in range(len(missing(rs[j], rs[j ^ 2]))):
            wait(leaving_z.at[j, i], zss.at[j, i])
        if j > 0:
            wait(summed.at[j], rts.at[j])
        if j < 2:
            wait(rows.at[j, 0], zos.at[j])

    @pl.when(is_home)
    def _():
        for i in range(1, 4):
            wait(packed.at[0], p3s.at[i])
        for i in range(1, NY * NC):
            wait(mixed.at[0], fs.at[i])

    @pl.when(jnp.logical_not(is_home))
    def _():
        wait(chunk(tok, y), p1s.at[0])
        wait(summed.at[0], rts.at[0])

    for i in range(NY):
        wait(owned.at[:, i * share:(i + 1) * share], fr.at[i])
    out[...] = owned[...]


def local(tokens, routes, gates, w_gate, w_up, w_down):
    tok_dev, width = tokens.shape
    hid = w_gate.shape[2]
    share = width // NY
    bf16, f32 = jnp.bfloat16, jnp.float32
    dma = pltpu.SemaphoreType.DMA
    hbm = pl.BlockSpec(memory_space=pltpu.HBM)
    return pl.pallas_call(
        kernel,
        out_shape=jax.ShapeDtypeStruct((tok_dev, width), bf16),
        in_specs=[hbm] * 6,
        out_specs=pl.BlockSpec(memory_space=pltpu.VMEM),
        scratch_shapes=[
            pltpu.VMEM((tok_dev, width), bf16),
            pltpu.VMEM((2, ROWS), jnp.int32),
            pltpu.VMEM((2, ROWS), f32),
            pltpu.VMEM((NY * NC, tok_dev, share), bf16),
            pltpu.VMEM((NC, width, hid), bf16),
            pltpu.VMEM((NC, width, hid), bf16),
            pltpu.VMEM((NC, hid, width), bf16),
            pltpu.VMEM((EXPERTS, ROWS, ROWS), bf16),
            pltpu.VMEM((EXPERTS, ROWS, ROWS), bf16),
            pltpu.VMEM((EXPERTS, ROWS, 128), f32),
            pltpu.VMEM((EXPERTS, CAP, share), bf16),
            pltpu.VMEM((BLOCKS, NY, CAP, share), bf16),
            pltpu.VMEM((BLOCKS, CAP, NC * hid), bf16),
            pltpu.VMEM((BLOCKS, NY, CAP, share), f32),
            pltpu.VMEM((BLOCKS, 2, 4, CAP, share), bf16),
            pltpu.VMEM((BLOCKS, 2, 4, CAP, share), bf16),
            pltpu.VMEM((BLOCKS, 3, CAP, share), bf16),
            pltpu.VMEM((BLOCKS, 3, CAP, share), bf16),
            pltpu.VMEM((BLOCKS, CAP, share), bf16),
            pltpu.VMEM((NZ, CAP, share), bf16),
            pltpu.VMEM((NY * NC, tok_dev, share), bf16),
            pltpu.VMEM((tok_dev, width), bf16),
            dma((NY,)), dma((NY * NC,)),
            dma((6,)), dma((3,)), dma((3,)),
            dma((4,)), dma((BLOCKS,)), dma((2,)),
            dma((BLOCKS, 2, 4)), dma((BLOCKS, 2, 4)),
            dma((BLOCKS, 3)), dma((BLOCKS, 3)),
            dma((BLOCKS, 2, 4)), dma((BLOCKS, 2, 4)),
            dma((BLOCKS, 3)), dma((BLOCKS, 3)),
            dma((BLOCKS,)), dma((NZ,)),
            dma((NY * NC,)), dma((NY,)),
        ],
        compiler_params=pltpu.CompilerParams(
            collective_id=0, has_side_effects=True, vmem_limit_bytes=62 * 2**20
        ),
        name="moe",
    )(tokens, routes.T, gates.T, w_gate, w_up, w_down)


def solution(mesh):
    return jax.shard_map(
        local,
        mesh=mesh,
        in_specs=(
            P(("dp", "exp", "tp"), None),
            P(("dp", "exp"), None),
            P(("dp", "exp"), None),
            P("exp", None, "tp"),
            P("exp", None, "tp"),
            P("exp", "tp", None),
        ),
        out_specs=P(("dp", "exp", "tp"), None),
        check_vma=False,
    )
```

time: 90 us -> 78.5 us (0.87)
  Pallas kernels: 88.4 us -> 76.9 us
    pallas_call x1, Pallas kernels: 88.4 us -> 76.9 us  [local(): pl.pallas_call(kernel, out_shape=jax.ShapeDtypeStruct((tok_dev, width), b...]
where the time goes in v2:
time: 78.5 us; the launch traced here: 78.4 us
  Pallas kernels  76.9 us (98%)
  local copies, waits for them, and re-layouts  1.42 us (2%)
    pallas_call x1, Pallas kernels, local(): pl.pallas_call(kernel, out_shape=jax.ShapeDtypeStruct((tok_dev, width), b...  76.9 us

profile of v2, /device:TPU:1, one launch (start us, length us, event | category | flops | bytes accessed | tf_op | source)
XLA Modules:
  0.0 78.4 jit_solution(17169335907496650649)
XLA Ops:
  0.0 76.9 %moe.1 = bf16[8,3072]{1,0:T(8,128)(2,1)} custom-call(bf16[8,3072]{1,0:T(8,128)(2,1)} %tok_in.1, s32[2,128]{1,0:T(2,128)} %bitcast.2, f32[2,128]{1,0:T(2,128)} %bitcast.3, bf16[1,3072,256]{2,1,0:T(8,128)(2,1)} %wg.1, bf16[1,3072,256]{2,1,0:T(8,128)(2,1)} %wu.1, bf16[1,256,3072]{2,1,0:T(8,128)(2,1)} %wd.1), custom_call_target="tpu_custom_call" | custom-call | tf_op jit(solution)/shard_map/moe/pallas_call | solution.py:403
  76.9 1.4 %copy.8 = bf16[8,3072]{1,0:T(8,128)(2,1)} copy(bf16[8,3072]{1,0:T(8,128)(2,1)} %moe.1) | data formatting | bytes 98304

commit v3 on v2

v3 whole, which is shorter than its diff:
```python
import jax
import jax.numpy as jnp
from jax import lax
from jax.experimental import pallas as pl
from jax.experimental.pallas import tpu as pltpu
from jax.sharding import PartitionSpec as P

MESH = pl.DeviceIdType.MESH
EXPERTS = 4
NZ = 8
NY = 8
NC = 2
ROWS = 128
CAP = 80
BLOCKS = NZ // NC
OFFSETS = ((0, 2, -2, 4), (1, 3, -1, -3))


HEAVY = (0, 1, 0, 1)


GROUPS = ((0, 2), (1, 3))
GATHER = (((0, 1, 2), (0, 1)), ((0, 1), (0, 1, 2)), ((0, 1, 2), (0, 1)), ((0, 1), (0, 1, 2)))
SCATTER = (((0, 1, 2), (0, 1)), ((0, 1), (0, 1, 2)), ((0, 1, 2), (0, 1)), ((0, 1), (0, 1, 2)))
ORDER = (
    ("ag", 0, 0, 1),
    ("ag", 0, 1, 1),
    ("ag", 2, 1, 1),
    ("ag", 2, 0, 1),
    ("ag", 0, 0, 2),
    ("zc", 2),
    ("ag", 1, 1, 1),
    ("ag", 2, 0, 2),
    ("ag", 1, 0, 1),
    ("ag", 2, 1, 2),
    ("zf", 2),
    ("zf", 0),
    ("ag", 3, 1, 1),
    ("prep",),
    ("zc", 0),
    ("ag", 0, 0, 3),
    ("ag", 2, 0, 3),
    ("ag", 0, 1, 2),
    ("ag", 3, 1, 2),
    ("ag", 1, 1, 2),
    ("zf", 1),
    ("zc", 1),
    ("ag", 3, 0, 1),
    ("zc", 3),
    ("zf", 3),
    ("up", 0, 0),
    ("ag", 1, 0, 2),
    ("ag", 3, 1, 3),
    ("ag", 1, 1, 3),
    ("ag", 3, 0, 2),
    ("up", 0, 1),
    ("down", 0, 0),
    ("down", 0, 1),
    ("rs", 2, 1, 2),
    ("rs", 0, 0, 3),
    ("zt", 0),
    ("rs", 0, 1, 2),
    ("rs", 2, 0, 3),
    ("up", 1, 0),
    ("up", 1, 1),
    ("down", 1, 0),
    ("down", 1, 1),
    ("rs", 3, 1, 3),
    ("rs", 1, 0, 2),
    ("rs", 1, 1, 3),
    ("zs", 0),
    ("rs", 3, 0, 2),
    ("rs", 2, 0, 2),
    ("zs", 1),
    ("rs", 3, 1, 2),
    ("zs", 3),
    ("rs", 1, 1, 2),
    ("rs", 3, 0, 1),
    ("zt", 1),
    ("zs", 2),
    ("rs", 0, 0, 2),
    ("rs", 3, 1, 1),
    ("rs", 2, 0, 1),
    ("rs", 2, 1, 1),
    ("rs", 1, 0, 1),
    ("zt", 3),
    ("rs", 1, 1, 1),
    ("fin", 3),
    ("rs", 0, 1, 1),
    ("rs", 0, 0, 1),
    ("zt", 2),
    ("fin", 2),
    ("fin", 1),
    ("fin", 0),
)


def kernel(
    tok_in, routes_in, gates_in, wg, wu, wd, out,
    tok, shares, routes, gates, arrived, gate_w, up_w, down_w, hot, back_hot, weight, packed, rows, hidden, partial,
    leaving, coming, leaving_z, coming_z, summed, returned, mixed, owned,
    p1s, p1r, lw, ws, wr, p3s, p3r, ags, agr, zcs, zcr, rss, rsr, zss, zsr, rts, rtr, fs, fr,
):
    groups, ag, rs, order = GROUPS, GATHER, SCATTER, ORDER
    z = lax.axis_index("exp")
    t = lax.axis_index("tp")
    y = t // NC
    c = lax.rem(t, NC)
    home_core = lax.rem(z, NC)
    side = lax.rem(z + c, NC)
    is_home = side == 0
    turn = 2 * home_core - 1
    share = rows.shape[-1]

    def at(zz, yy, cc):
        return {"exp": zz, "tp": yy * NC + cc}

    def ring(v, n):
        return lax.rem(v + n, n)

    def send(src, dst, ssem, rsem, device):
        pltpu.make_async_remote_copy(
            src_ref=src, dst_ref=dst, send_sem=ssem, recv_sem=rsem, device_id=device, device_id_type=MESH
        ).start()

    def wait(ref, sem):
        pltpu.make_async_copy(ref, ref, sem).wait()

    def chunk(ref, index):
        return ref.at[:, pl.ds(pl.multiple_of(index * share, 128), share)]

    def center(j):
        return ring(y + j // 2 * (NY // 2), NY)

    def near(j, way, d):
        return ring(center(j) + (1 - 2 * way) * d, NY)

    partner = z - turn
    weights = ((wg, gate_w), (wu, up_w), (wd, down_w))
    small = ((tok_in, tok), (routes_in, routes), (gates_in, gates))
    for i, (src, dst) in enumerate(small):
        pltpu.make_async_copy(src, dst, lw.at[3 + i]).start()
    barrier = pltpu.get_barrier_semaphore()
    for dy in (4, 3, 5, 2, 6, 1, 7, 0):
        for dc in range(NC):
            if dy or dc:
                pl.semaphore_signal(
                    barrier, inc=1, device_id=at(z, ring(y + dy, NY), ring(c + dc, NC)), device_id_type=MESH
                )
    for dz in (4, 3, 5, 2, 6, 1, 7):
        pl.semaphore_signal(barrier, inc=1, device_id=at(ring(z + dz, NZ), y, c), device_id_type=MESH)
    for i, (src, dst) in enumerate(weights):
        pltpu.make_async_copy(src.at[0], dst.at[c], lw.at[i]).start()
    wait(tok, lw.at[3])
    pl.semaphore_wait(barrier, NY * NC - 1 + NZ - 1)

    for f in range(NY):
        g = (f + NY // 2) % NY
        shares[f, :, :share] = tok[:, f * share:(f + 1) * share]
        shares[f, :, share:] = tok[:, g * share:(g + 1) * share]

    for dy in (4, 3, 5, 2, 6, 1, 7):
        to = ring(y + dy, NY)
        send(shares.at[to], arrived.at[t], p1s.at[dy], p1r, at(z, to, home_core))

    @pl.when(is_home)
    def _():
        pltpu.make_async_copy(shares.at[y], arrived.at[t], p1r).start()

    @pl.when(jnp.logical_not(is_home))
    def _():
        send(shares.at[y], arrived.at[t], p1s.at[0], p1r, at(z, y, home_core))

    for i, (src, dst) in enumerate(weights):
        send(src.at[0], dst.at[c], ws.at[i], wr.at[i], at(z, y, 1 - c))

    for i, (src, dst) in enumerate(small[1:]):
        wait(dst, lw.at[4 + i])

    def pick(e, first, second):
        here = [jnp.broadcast_to(routes[k:k + 1, :], (ROWS, ROWS)) == e for k in range(2)]
        return jnp.where(here[0], first, 0.0) + jnp.where(here[1], second, 0.0)

    @pl.when(is_home)
    def _():
        row_ids = lax.broadcasted_iota(jnp.int32, (ROWS, ROWS), 0)
        col_ids = lax.broadcasted_iota(jnp.int32, (ROWS, ROWS), 1)
        earlier = jnp.where(row_ids < col_ids, 1.0, 0.0).astype(jnp.bfloat16)
        slots = row_ids.astype(jnp.float32)
        for e in range(EXPERTS):
            mine = pick(e, 1.0, 1.0)
            before = jnp.dot(mine.astype(jnp.bfloat16), earlier, preferred_element_type=jnp.float32)
            placed = jnp.where(before == slots, mine, 0.0)
            hot[e] = placed.astype(jnp.bfloat16)
        wait(arrived, p1r)
        block = arrived[...].astype(jnp.float32).reshape(ROWS, 2 * share).astype(jnp.bfloat16)
        for j, k in ((0, 0), (0, 1), (2, 1), (3, 0), (3, 1), (2, 0), (1, 1), (1, 0)):
            to = ring(z - turn * OFFSETS[0][j], NZ) if k == 0 else ring(z + turn * OFFSETS[1][j], NZ)
            e, lo = to // (NZ // EXPERTS), j // 2 * share
            slot = k * BLOCKS + j
            packed[slot] = jnp.dot(
                hot[e, :CAP, :], block[:, lo:lo + share], preferred_element_type=jnp.float32
            ).astype(jnp.bfloat16)
            if slot == 0:
                pltpu.make_async_copy(packed.at[slot], rows.at[j, center(j)], p3r.at[j]).start()
            else:
                send(packed.at[slot], rows.at[j, center(j)], p3s.at[slot], p3r.at[j], at(to, y, c))

    waited = set()

    def need(kind, j, *where):
        key = (kind, j) + where
        if key in waited:
            return
        waited.add(key)
        if kind == "p3":
            wait(rows.at[j, center(j)], p3r.at[j])
        elif kind == "ag":
            way, d = where
            wait(rows.at[j, near(j, way, -d)], agr.at[j, way, d - 1])
        elif kind == "zc":
            wait(rows.at[j, center(j ^ 2)], zcr.at[j, 0])
        elif kind == "zf":
            wait(rows.at[j, near(j ^ 2, HEAVY[j], -1)], zcr.at[j, 1])
        elif kind == "rs":
            way, d = where
            wait(coming.at[j, way, d - 1], rsr.at[j, way, d - 1])
        else:
            wait(coming_z.at[j, where[0]], zsr.at[j, where[0]])

    def gather(j, way, d):
        parent = ag[j][way][d - 1]
        piece = rows.at[j, near(j, way, -parent)]
        need("ag", j, way, parent) if parent else need("p3", j)
        to = ring(y + (1 - 2 * way) * (d - parent), NY)
        send(piece, piece, ags.at[j, way, d - 1], agr.at[j, way, d - 1], at(z, to, c))

    def share_center(j):
        need("p3", j)
        f = center(j)
        send(rows.at[j, f], rows.at[j ^ 2, f], zcs.at[j, 0], zcr.at[j ^ 2, 0], at(partner, y, c))

    def share_next(j):
        need("ag", j, HEAVY[j], 1)
        f = near(j, HEAVY[j], -1)
        send(rows.at[j, f], rows.at[j ^ 2, f], zcs.at[j, 1], zcr.at[j ^ 2, 1], at(partner, y, c))

    def up(g, core):
        if core == 0:
            for j in groups[g]:
                need("p3", j)
                for way in range(2):
                    for d in range(1, len(ag[j][way]) + 1):
                        need("ag", j, way, d)
                need("zc", j)
                need("zf", j)
        if "up" not in waited:
            waited.add("up")
            for i, (src, dst) in enumerate(weights[:2]):
                wait(dst.at[c], lw.at[i])
                wait(dst.at[1 - c], wr.at[i])
        x = jnp.concatenate(
            [jnp.concatenate([rows[j, f] for f in range(NY)], axis=1) for j in groups[g]], axis=0
        )
        gp = jnp.dot(x, gate_w[core], preferred_element_type=jnp.float32)
        u = jnp.dot(x, up_w[core], preferred_element_type=jnp.float32)
        n = gp.shape[1]
        hid = (gp / (1.0 + jnp.exp(-gp)) * u).astype(jnp.bfloat16)
        for i, j in enumerate(groups[g]):
            hidden[j, :, core * n:(core + 1) * n] = hid[i * CAP:(i + 1) * CAP]

    def down(g, half):
        if "down" not in waited:
            waited.add("down")
            wait(down_w.at[c], lw.at[2])
            wait(down_w.at[1 - c], wr.at[2])
        n = down_w.shape[1]
        h = jnp.concatenate([hidden[j] for j in groups[g]], axis=0)
        for f in range(half * NY // 2, (half + 1) * NY // 2, 2):
            lo, hi = f * share, (f + 2) * share
            r = jnp.dot(h[:, :n], down_w[0, :, lo:hi], preferred_element_type=jnp.float32)
            r += jnp.dot(h[:, n:], down_w[1, :, lo:hi], preferred_element_type=jnp.float32)
            for i, j in enumerate(groups[g]):
                partial[j, f] = r[i * CAP:(i + 1) * CAP, :share]
                partial[j, f + 1] = r[i * CAP:(i + 1) * CAP, share:]

    def across(j, i):
        f = center(j ^ 2) if i else near(j ^ 2, HEAVY[j], 1)
        leaving_z[j, i] = partial[j, f].astype(jnp.bfloat16)
        send(leaving_z.at[j, i], coming_z.at[j ^ 2, i], zss.at[j, i], zsr.at[j ^ 2, i], at(partner, y, c))

    def scatter(j, way, d):
        total = partial[j, near(j, way, d)]
        if (way, d) == (HEAVY[j], 1):
            need("zs", j, 0)
            total = total + coming_z[j, 0].astype(jnp.float32)
        total = total + children(j, way, d)
        leaving[j, way, d - 1] = total.astype(jnp.bfloat16)
        to = ring(y + (1 - 2 * way) * (d - rs[j][way][d - 1]), NY)
        send(
            leaving.at[j, way, d - 1], coming.at[j, way, d - 1], rss.at[j, way, d - 1], rsr.at[j, way, d - 1],
            at(z, to, c),
        )

    def children(j, way, d):
        total = 0.0
        for e, parent in enumerate(rs[j][way], 1):
            if parent == d:
                need("rs", j, way, e)
                total = total + coming[j, way, e - 1].astype(jnp.float32)
        return total

    def finish(j):
        need("zs", j, 1)
        total = partial[j, center(j)] + coming_z[j, 1].astype(jnp.float32)
        for way in range(2):
            total = total + children(j, way, 0)
        summed[j] = total.astype(jnp.bfloat16)
        back = ring(z + turn * (OFFSETS[0][j] + side * (OFFSETS[1][j] - OFFSETS[0][j])), NZ)
        if j == 0:
            @pl.when(is_home)
            def _():
                pltpu.make_async_copy(summed.at[j], returned.at[z], rtr.at[z]).start()

            @pl.when(jnp.logical_not(is_home))
            def _():
                send(summed.at[j], returned.at[z], rts.at[j], rtr.at[z], at(back, y, c))
        else:
            send(summed.at[j], returned.at[z], rts.at[j], rtr.at[z], at(back, y, c))

    def prepare():
        @pl.when(is_home)
        def _():
            row_ids = lax.broadcasted_iota(jnp.int32, (ROWS, ROWS), 0)
            col_ids = lax.broadcasted_iota(jnp.int32, (ROWS, ROWS), 1)
            g0, g1 = (jnp.broadcast_to(gates[k:k + 1, :], (ROWS, ROWS)) for k in range(2))
            for e in range(EXPERTS):
                back_hot[e] = hot[e].astype(jnp.float32).T.astype(jnp.bfloat16)
                gate = jnp.sum(jnp.where(row_ids == col_ids, pick(e, g0, g1), 0.0), axis=1, keepdims=True)
                weight[e] = jnp.broadcast_to(gate, (ROWS, 128))

    def across_next(j):
        across(j, 0)

    def across_center(j):
        across(j, 1)

    step = {"zs": across_next, "zt": across_center, "prep": prepare, "ag": gather, "zc": share_center, "zf": share_next, "up": up, "down": down, "rs": scatter, "fin": finish}
    for task in order:
        step[task[0]](*task[1:])

    @pl.when(is_home)
    def _():
        totals = [jnp.zeros((ROWS, share), jnp.float32)] * 2
        for j in [task[1] for task in order if task[0] == "fin"]:
            for k in range(2):
                to = ring(z - turn * OFFSETS[0][j], NZ) if k == 0 else ring(z + turn * OFFSETS[1][j], NZ)
                e = to // (NZ // EXPERTS)
                wait(returned.at[to], rtr.at[to])
                picked = jnp.dot(back_hot[e, :, :CAP], returned[to], preferred_element_type=jnp.float32)
                totals[j // 2] += jnp.concatenate([weight[e]] * (share // 128), axis=1) * picked
        for i in range(2):
            mixed[:, :, i * share:(i + 1) * share] = totals[i].reshape(
                NY * NC, ROWS // (NY * NC), share
            ).astype(jnp.bfloat16)
        for dy in (4, 3, 5, 2, 6, 1, 7, 0):
            for dc in range(NC):
                to, core = ring(y + dy, NY), ring(c + dc, NC)
                src = mixed.at[to * NC + core]
                if dy == 0 and dc == 0:
                    pltpu.make_async_copy(src, owned.at[y], fr).start()
                else:
                    send(src, owned.at[y], fs.at[dy * NC + dc], fr, at(z, to, core))

    for dy in range(1, NY):
        wait(shares.at[0], p1s.at[dy])
    for i, (src, dst) in enumerate(weights):
        wait(src.at[0], ws.at[i])
    for j in range(BLOCKS):
        for way in range(2):
            for h in range(len(ag[j][way])):
                wait(rows.at[j, 0], ags.at[j, way, h])
            for h in range(len(rs[j][way])):
                wait(leaving.at[j, way, h], rss.at[j, way, h])
        for i in range(2):
            wait(rows.at[j, 0], zcs.at[j, i])
            wait(leaving_z.at[j, i], zss.at[j, i])
        if j > 0:
            wait(summed.at[j], rts.at[j])

    @pl.when(is_home)
    def _():
        for i in range(1, 2 * BLOCKS):
            wait(packed.at[0], p3s.at[i])
        for i in range(1, NY * NC):
            wait(mixed.at[0], fs.at[i])

    @pl.when(jnp.logical_not(is_home))
    def _():
        wait(shares.at[0], p1s.at[0])
        wait(summed.at[0], rts.at[0])

    wait(owned, fr)
    for f in range(NY):
        both = owned[f, :, :share].astype(jnp.float32)
        both += owned[(f + NY // 2) % NY, :, share:].astype(jnp.float32)
        out[:, f * share:(f + 1) * share] = both.astype(jnp.bfloat16)


def local(tokens, routes, gates, w_gate, w_up, w_down):
    tok_dev, width = tokens.shape
    hid = w_gate.shape[2]
    share = width // NY
    bf16, f32 = jnp.bfloat16, jnp.float32
    dma = pltpu.SemaphoreType.DMA
    hbm = pl.BlockSpec(memory_space=pltpu.HBM)
    return pl.pallas_call(
        kernel,
        out_shape=jax.ShapeDtypeStruct((tok_dev, width), bf16),
        in_specs=[hbm] * 6,
        out_specs=pl.BlockSpec(memory_space=pltpu.VMEM),
        scratch_shapes=[
            pltpu.VMEM((tok_dev, width), bf16),
            pltpu.VMEM((NY, tok_dev, 2 * share), bf16),
            pltpu.VMEM((2, ROWS), jnp.int32),
            pltpu.VMEM((2, ROWS), f32),
            pltpu.VMEM((NY * NC, tok_dev, 2 * share), bf16),
            pltpu.VMEM((NC, width, hid), bf16),
            pltpu.VMEM((NC, width, hid), bf16),
            pltpu.VMEM((NC, hid, width), bf16),
            pltpu.VMEM((EXPERTS, ROWS, ROWS), bf16),
            pltpu.VMEM((EXPERTS, ROWS, ROWS), bf16),
            pltpu.VMEM((EXPERTS, ROWS, 128), f32),
            pltpu.VMEM((2 * BLOCKS, CAP, share), bf16),
            pltpu.VMEM((BLOCKS, NY, CAP, share), bf16),
            pltpu.VMEM((BLOCKS, CAP, NC * hid), bf16),
            pltpu.VMEM((BLOCKS, NY, CAP, share), f32),
            pltpu.VMEM((BLOCKS, 2, 3, CAP, share), bf16),
            pltpu.VMEM((BLOCKS, 2, 3, CAP, share), bf16),
            pltpu.VMEM((BLOCKS, 2, CAP, share), bf16),
            pltpu.VMEM((BLOCKS, 2, CAP, share), bf16),
            pltpu.VMEM((BLOCKS, CAP, share), bf16),
            pltpu.VMEM((NZ, CAP, share), bf16),
            pltpu.VMEM((NY * NC, tok_dev, 2 * share), bf16),
            pltpu.VMEM((NY, tok_dev, 2 * share), bf16),
            dma((NY,)), dma,
            dma((6,)), dma((3,)), dma((3,)),
            dma((2 * BLOCKS,)), dma((BLOCKS,)),
            dma((BLOCKS, 2, 3)), dma((BLOCKS, 2, 3)),
            dma((BLOCKS, 2)), dma((BLOCKS, 2)),
            dma((BLOCKS, 2, 3)), dma((BLOCKS, 2, 3)),
            dma((BLOCKS, 2)), dma((BLOCKS, 2)),
            dma((BLOCKS,)), dma((NZ,)),
            dma((NY * NC,)), dma,
        ],
        compiler_params=pltpu.CompilerParams(
            collective_id=0, has_side_effects=True, vmem_limit_bytes=62 * 2**20
        ),
        name="moe",
    )(tokens, routes.T, gates.T, w_gate, w_up, w_down)


def solution(mesh):
    return jax.shard_map(
        local,
        mesh=mesh,
        in_specs=(
            P(("dp", "exp", "tp"), None),
            P(("dp", "exp"), None),
            P(("dp", "exp"), None),
            P("exp", None, "tp"),
            P("exp", None, "tp"),
            P("exp", "tp", None),
        ),
        out_specs=P(("dp", "exp", "tp"), None),
        check_vma=False,
    )
```

time: 78.5 us -> 75.1 us (0.957)
  Pallas kernels: 76.9 us -> 73.5 us
    pallas_call x1, Pallas kernels: 76.9 us -> 73.5 us  [local(): pl.pallas_call(kernel, out_shape=jax.ShapeDtypeStruct((tok_dev, width), b...]
where the time goes in v3:
time: 75.1 us; the launch traced here: 74.9 us
  Pallas kernels  73.5 us (98%)
  local copies, waits for them, and re-layouts  1.42 us (2%)
    pallas_call x1, Pallas kernels, local(): pl.pallas_call(kernel, out_shape=jax.ShapeDtypeStruct((tok_dev, width), b...  73.5 us

profile of v3, /device:TPU:1, one launch (start us, length us, event | category | flops | bytes accessed | tf_op | source)
XLA Modules:
  0.0 74.9 jit_solution(14708799728368855850)
XLA Ops:
  0.0 73.5 %moe.1 = bf16[8,3072]{1,0:T(8,128)(2,1)} custom-call(bf16[8,3072]{1,0:T(8,128)(2,1)} %tok_in.1, s32[2,128]{1,0:T(2,128)} %bitcast.2, f32[2,128]{1,0:T(2,128)} %bitcast.3, bf16[1,3072,256]{2,1,0:T(8,128)(2,1)} %wg.1, bf16[1,3072,256]{2,1,0:T(8,128)(2,1)} %wu.1, bf16[1,256,3072]{2,1,0:T(8,128)(2,1)} %wd.1), custom_call_target="tpu_custom_call" | custom-call | tf_op jit(solution)/shard_map/moe/pallas_call | solution.py:417
  73.5 1.4 %copy.8 = bf16[8,3072]{1,0:T(8,128)(2,1)} copy(bf16[8,3072]{1,0:T(8,128)(2,1)} %moe.1) | data formatting | bytes 98304

commit v4 on v3

--- a/solution.py
+++ b/solution.py
@@ -21,75 +21,75 @@
 
 GROUPS = ((0, 2), (1, 3))
 GATHER = (((0, 1, 2), (0, 1)), ((0, 1), (0, 1, 2)), ((0, 1, 2), (0, 1)), ((0, 1), (0, 1, 2)))
-SCATTER = (((0, 1, 2), (0, 1)), ((0, 1), (0, 1, 2)), ((0, 1, 2), (0, 1)), ((0, 1), (0, 1, 2)))
+SCATTER = (((0, 1, 2), (0, 1)), ((0, 1), (0, 1)), ((0, 1, 2), (0, 1)), ((0, 1), (0, 1)))
 ORDER = (
     ("ag", 0, 0, 1),
     ("ag", 0, 1, 1),
+    ("prep",),
+    ("zc", 0),
+    ("ag", 2, 0, 1),
     ("ag", 2, 1, 1),
-    ("ag", 2, 0, 1),
+    ("zc", 2),
     ("ag", 0, 0, 2),
-    ("zc", 2),
     ("ag", 1, 1, 1),
+    ("ag", 1, 0, 1),
+    ("ag", 3, 1, 1),
     ("ag", 2, 0, 2),
-    ("ag", 1, 0, 1),
-    ("ag", 2, 1, 2),
+    ("ag", 0, 1, 2),
+    ("ag", 0, 0, 3),
     ("zf", 2),
     ("zf", 0),
-    ("ag", 3, 1, 1),
-    ("prep",),
-    ("zc", 0),
-    ("ag", 0, 0, 3),
+    ("ag", 1, 1, 2),
+    ("ag", 3, 0, 1),
+    ("zc", 1),
+    ("ag", 2, 1, 2),
     ("ag", 2, 0, 3),
-    ("ag", 0, 1, 2),
+    ("zc", 3),
+    ("ag", 1, 0, 2),
+    ("zf", 1),
     ("ag", 3, 1, 2),
-    ("ag", 1, 1, 2),
-    ("zf", 1),
-    ("zc", 1),
-    ("ag", 3, 0, 1),
-    ("zc", 3),
+    ("ag", 1, 1, 3),
     ("zf", 3),
     ("up", 0, 0),
-    ("ag", 1, 0, 2),
+    ("ag", 3, 0, 2),
     ("ag", 3, 1, 3),
-    ("ag", 1, 1, 3),
-    ("ag", 3, 0, 2),
     ("up", 0, 1),
     ("down", 0, 0),
     ("down", 0, 1),
-    ("rs", 2, 1, 2),
-    ("rs", 0, 0, 3),
     ("zt", 0),
     ("rs", 0, 1, 2),
+    ("rs", 2, 1, 2),
     ("rs", 2, 0, 3),
+    ("zs", 2),
+    ("zs", 0),
+    ("rs", 0, 0, 3),
     ("up", 1, 0),
     ("up", 1, 1),
     ("down", 1, 0),
     ("down", 1, 1),
-    ("rs", 3, 1, 3),
     ("rs", 1, 0, 2),
-    ("rs", 1, 1, 3),
-    ("zs", 0),
-    ("rs", 3, 0, 2),
+    ("zu", 3),
     ("rs", 2, 0, 2),
     ("zs", 1),
+    ("rs", 3, 0, 2),
     ("rs", 3, 1, 2),
+    ("zu", 1),
+    ("rs", 0, 1, 1),
     ("zs", 3),
+    ("rs", 0, 0, 2),
     ("rs", 1, 1, 2),
+    ("rs", 2, 1, 1),
+    ("zt", 1),
+    ("rs", 2, 0, 1),
+    ("rs", 3, 1, 1),
     ("rs", 3, 0, 1),
-    ("zt", 1),
-    ("zs", 2),
-    ("rs", 0, 0, 2),
-    ("rs", 3, 1, 1),
-    ("rs", 2, 0, 1),
-    ("rs", 2, 1, 1),
+    ("zt", 3),
     ("rs", 1, 0, 1),
-    ("zt", 3),
     ("rs", 1, 1, 1),
-    ("fin", 3),
-    ("rs", 0, 1, 1),
     ("rs", 0, 0, 1),
     ("zt", 2),
     ("fin", 2),
+    ("fin", 3),
     ("fin", 1),
     ("fin", 0),
 )
@@ -206,6 +206,9 @@
             else:
                 send(packed.at[slot], rows.at[j, center(j)], p3s.at[slot], p3r.at[j], at(to, y, c))
 
+    def short(rings, j, way):
+        return len(rings[j][way]) == 2
+
     waited = set()
 
     def need(kind, j, *where):
@@ -222,6 +225,8 @@
             wait(rows.at[j, center(j ^ 2)], zcr.at[j, 0])
         elif kind == "zf":
             wait(rows.at[j, near(j ^ 2, HEAVY[j], -1)], zcr.at[j, 1])
+        elif kind == "zg":
+            wait(rows.at[j, near(j ^ 2, 1 - HEAVY[j], -1)], zcr.at[j, 2])
         elif kind == "rs":
             way, d = where
             wait(coming.at[j, way, d - 1], rsr.at[j, way, d - 1])
@@ -240,10 +245,10 @@
         f = center(j)
         send(rows.at[j, f], rows.at[j ^ 2, f], zcs.at[j, 0], zcr.at[j ^ 2, 0], at(partner, y, c))
 
-    def share_next(j):
-        need("ag", j, HEAVY[j], 1)
-        f = near(j, HEAVY[j], -1)
-        send(rows.at[j, f], rows.at[j ^ 2, f], zcs.at[j, 1], zcr.at[j ^ 2, 1], at(partner, y, c))
+    def share_near(j, way, i):
+        need("ag", j, way, 1)
+        f = near(j, way, -1)
+        send(rows.at[j, f], rows.at[j ^ 2, f], zcs.at[j, i], zcr.at[j ^ 2, i], at(partner, y, c))
 
     def up(g, core):
         if core == 0:
@@ -253,7 +258,10 @@
                     for d in range(1, len(ag[j][way]) + 1):
                         need("ag", j, way, d)
                 need("zc", j)
-                need("zf", j)
+                if short(ag, j, 1 - HEAVY[j]):
+                    need("zf", j)
+                if short(ag, j, HEAVY[j]):
+                    need("zg", j)
         if "up" not in waited:
             waited.add("up")
             for i, (src, dst) in enumerate(weights[:2]):
@@ -285,15 +293,16 @@
                 partial[j, f + 1] = r[i * CAP:(i + 1) * CAP, share:]
 
     def across(j, i):
-        f = center(j ^ 2) if i else near(j ^ 2, HEAVY[j], 1)
+        f = center(j ^ 2) if i == 1 else near(j ^ 2, HEAVY[j] if i == 0 else 1 - HEAVY[j], 1)
         leaving_z[j, i] = partial[j, f].astype(jnp.bfloat16)
         send(leaving_z.at[j, i], coming_z.at[j ^ 2, i], zss.at[j, i], zsr.at[j ^ 2, i], at(partner, y, c))
 
     def scatter(j, way, d):
         total = partial[j, near(j, way, d)]
-        if (way, d) == (HEAVY[j], 1):
-            need("zs", j, 0)
-            total = total + coming_z[j, 0].astype(jnp.float32)
+        if d == 1 and short(rs, j, 1 - way):
+            i = 0 if way == HEAVY[j] else 2
+            need("zs", j, i)
+            total = total + coming_z[j, i].astype(jnp.float32)
         total = total + children(j, way, d)
         leaving[j, way, d - 1] = total.astype(jnp.bfloat16)
         to = ring(y + (1 - 2 * way) * (d - rs[j][way][d - 1]), NY)
@@ -339,13 +348,10 @@
                 gate = jnp.sum(jnp.where(row_ids == col_ids, pick(e, g0, g1), 0.0), axis=1, keepdims=True)
                 weight[e] = jnp.broadcast_to(gate, (ROWS, 128))
 
-    def across_next(j):
-        across(j, 0)
-
-    def across_center(j):
-        across(j, 1)
-
-    step = {"zs": across_next, "zt": across_center, "prep": prepare, "ag": gather, "zc": share_center, "zf": share_next, "up": up, "down": down, "rs": scatter, "fin": finish}
+    step = {
+        "zf": lambda j: share_near(j, HEAVY[j], 1), "zg": lambda j: share_near(j, 1 - HEAVY[j], 2),
+        "zs": lambda j: across(j, 0), "zt": lambda j: across(j, 1), "zu": lambda j: across(j, 2), "prep": prepare,
+        "ag": gather, "zc": share_center, "up": up, "down": down, "rs": scatter, "fin": finish}
     for task in order:
         step[task[0]](*task[1:])
 
@@ -382,9 +388,12 @@
                 wait(rows.at[j, 0], ags.at[j, way, h])
             for h in range(len(rs[j][way])):
                 wait(leaving.at[j, way, h], rss.at[j, way, h])
-        for i in range(2):
-            wait(rows.at[j, 0], zcs.at[j, i])
-            wait(leaving_z.at[j, i], zss.at[j, i])
+        for i, way in enumerate((None, 1 - HEAVY[j], HEAVY[j])):
+            if way is None or short(ag, j, way):
+                wait(rows.at[j, 0], zcs.at[j, i])
+        for i, way in enumerate((1 - HEAVY[j], None, HEAVY[j])):
+            if way is None or short(rs, j, way):
+                wait(leaving_z.at[j, i], zss.at[j, i])
         if j > 0:
             wait(summed.at[j], rts.at[j])
 
@@ -437,8 +446,8 @@
             pltpu.VMEM((BLOCKS, NY, CAP, share), f32),
             pltpu.VMEM((BLOCKS, 2, 3, CAP, share), bf16),
             pltpu.VMEM((BLOCKS, 2, 3, CAP, share), bf16),
-            pltpu.VMEM((BLOCKS, 2, CAP, share), bf16),
-            pltpu.VMEM((BLOCKS, 2, CAP, share), bf16),
+            pltpu.VMEM((BLOCKS, 3, CAP, share), bf16),
+            pltpu.VMEM((BLOCKS, 3, CAP, share), bf16),
             pltpu.VMEM((BLOCKS, CAP, share), bf16),
             pltpu.VMEM((NZ, CAP, share), bf16),
             pltpu.VMEM((NY * NC, tok_dev, 2 * share), bf16),
@@ -447,9 +456,9 @@
             dma((6,)), dma((3,)), dma((3,)),
             dma((2 * BLOCKS,)), dma((BLOCKS,)),
             dma((BLOCKS, 2, 3)), dma((BLOCKS, 2, 3)),
-            dma((BLOCKS, 2)), dma((BLOCKS, 2)),
+            dma((BLOCKS, 3)), dma((BLOCKS, 3)),
             dma((BLOCKS, 2, 3)), dma((BLOCKS, 2, 3)),
-            dma((BLOCKS, 2)), dma((BLOCKS, 2)),
+            dma((BLOCKS, 3)), dma((BLOCKS, 3)),
             dma((BLOCKS,)), dma((NZ,)),
             dma((NY * NC,)), dma,
         ],

time: 75.1 us -> 72.4 us (0.964)
  Pallas kernels: 73.5 us -> 70.8 us
    pallas_call x1, Pallas kernels: 73.5 us -> 70.8 us  [local(): pl.pallas_call(kernel, out_shape=jax.ShapeDtypeStruct((tok_dev, width), b...]
where the time goes in v4:
time: 72.4 us; the launch traced here: 72.2 us
  Pallas kernels  70.8 us (98%)
  local copies, waits for them, and re-layouts  1.42 us (2%)
    pallas_call x1, Pallas kernels, local(): pl.pallas_call(kernel, out_shape=jax.ShapeDtypeStruct((tok_dev, width), b...  70.8 us

profile of v4, /device:TPU:1, one launch (start us, length us, event | category | flops | bytes accessed | tf_op | source)
XLA Modules:
  0.0 72.2 jit_solution(11206019151688697452)
XLA Ops:
  0.0 70.8 %moe.1 = bf16[8,3072]{1,0:T(8,128)(2,1)} custom-call(bf16[8,3072]{1,0:T(8,128)(2,1)} %tok_in.1, s32[2,128]{1,0:T(2,128)} %bitcast.2, f32[2,128]{1,0:T(2,128)} %bitcast.3, bf16[1,3072,256]{2,1,0:T(8,128)(2,1)} %wg.1, bf16[1,3072,256]{2,1,0:T(8,128)(2,1)} %wu.1, bf16[1,256,3072]{2,1,0:T(8,128)(2,1)} %wd.1), custom_call_target="tpu_custom_call" | custom-call | tf_op jit(solution)/shard_map/moe/pallas_call | solution.py:426
  70.8 1.4 %copy.8 = bf16[8,3072]{1,0:T(8,128)(2,1)} copy(bf16[8,3072]{1,0:T(8,128)(2,1)} %moe.1) | data formatting | bytes 98304

commit v5 on v4

--- a/solution.py
+++ b/solution.py
@@ -138,26 +138,21 @@
     partner = z - turn
     weights = ((wg, gate_w), (wu, up_w), (wd, down_w))
     small = ((tok_in, tok), (routes_in, routes), (gates_in, gates))
+    barrier = pltpu.get_barrier_semaphore()
+    for d in (4, 3, 5, 2, 6, 1, 7, 0):
+        peers = [at(z, ring(y + d, NY), c), at(z, ring(y + d, NY), 1 - c), at(ring(z + d, NZ), y, c)]
+        for peer in peers if d else peers[1:2]:
+            pl.semaphore_signal(barrier, inc=1, device_id=peer, device_id_type=MESH)
     for i, (src, dst) in enumerate(small):
         pltpu.make_async_copy(src, dst, lw.at[3 + i]).start()
-    barrier = pltpu.get_barrier_semaphore()
-    for dy in (4, 3, 5, 2, 6, 1, 7, 0):
-        for dc in range(NC):
-            if dy or dc:
-                pl.semaphore_signal(
-                    barrier, inc=1, device_id=at(z, ring(y + dy, NY), ring(c + dc, NC)), device_id_type=MESH
-                )
-    for dz in (4, 3, 5, 2, 6, 1, 7):
-        pl.semaphore_signal(barrier, inc=1, device_id=at(ring(z + dz, NZ), y, c), device_id_type=MESH)
     for i, (src, dst) in enumerate(weights):
         pltpu.make_async_copy(src.at[0], dst.at[c], lw.at[i]).start()
     wait(tok, lw.at[3])
-    pl.semaphore_wait(barrier, NY * NC - 1 + NZ - 1)
-
     for f in range(NY):
         g = (f + NY // 2) % NY
         shares[f, :, :share] = tok[:, f * share:(f + 1) * share]
         shares[f, :, share:] = tok[:, g * share:(g + 1) * share]
+    pl.semaphore_wait(barrier, NY * NC - 1 + NZ - 1)
 
     for dy in (4, 3, 5, 2, 6, 1, 7):
         to = ring(y + dy, NY)
@@ -194,17 +189,19 @@
             hot[e] = placed.astype(jnp.bfloat16)
         wait(arrived, p1r)
         block = arrived[...].astype(jnp.float32).reshape(ROWS, 2 * share).astype(jnp.bfloat16)
+        every = hot[:, :CAP, :].reshape(EXPERTS * CAP, ROWS)
+        for i in range(2):
+            packed[i] = jnp.dot(
+                every, block[:, i * share:(i + 1) * share], preferred_element_type=jnp.float32
+            ).reshape(EXPERTS, CAP, share).astype(jnp.bfloat16)
         for j, k in ((0, 0), (0, 1), (2, 1), (3, 0), (3, 1), (2, 0), (1, 1), (1, 0)):
             to = ring(z - turn * OFFSETS[0][j], NZ) if k == 0 else ring(z + turn * OFFSETS[1][j], NZ)
-            e, lo = to // (NZ // EXPERTS), j // 2 * share
+            src = packed.at[j // 2, to // (NZ // EXPERTS)]
             slot = k * BLOCKS + j
-            packed[slot] = jnp.dot(
-                hot[e, :CAP, :], block[:, lo:lo + share], preferred_element_type=jnp.float32
-            ).astype(jnp.bfloat16)
             if slot == 0:
-                pltpu.make_async_copy(packed.at[slot], rows.at[j, center(j)], p3r.at[j]).start()
+                pltpu.make_async_copy(src, rows.at[j, center(j)], p3r.at[j]).start()
             else:
-                send(packed.at[slot], rows.at[j, center(j)], p3s.at[slot], p3r.at[j], at(to, y, c))
+                send(src, rows.at[j, center(j)], p3s.at[slot], p3r.at[j], at(to, y, c))
 
     def short(rings, j, way):
         return len(rings[j][way]) == 2
@@ -355,6 +352,32 @@
     for task in order:
         step[task[0]](*task[1:])
 
+    for dy in range(1, NY):
+        wait(shares.at[0], p1s.at[dy])
+    for i, (src, dst) in enumerate(weights):
+        wait(src.at[0], ws.at[i])
+    for j in range(BLOCKS):
+        for way in range(2):
+            for h in range(len(ag[j][way])):
+                wait(rows.at[j, 0], ags.at[j, way, h])
+            for h in range(len(rs[j][way])):
+                wait(leaving.at[j, way, h], rss.at[j, way, h])
+        for i, way in enumerate((None, 1 - HEAVY[j], HEAVY[j])):
+            if way is None or short(ag, j, way):
+                wait(rows.at[j, 0], zcs.at[j, i])
+        for i, way in enumerate((1 - HEAVY[j], None, HEAVY[j])):
+            if way is None or short(rs, j, way):
+                wait(leaving_z.at[j, i], zss.at[j, i])
+
+    @pl.when(is_home)
+    def _():
+        for i in range(1, 2 * BLOCKS):
+            wait(packed.at[0, 0], p3s.at[i])
+
+    @pl.when(jnp.logical_not(is_home))
+    def _():
+        wait(shares.at[0], p1s.at[0])
+
     @pl.when(is_home)
     def _():
         totals = [jnp.zeros((ROWS, share), jnp.float32)] * 2
@@ -378,35 +401,17 @@
                 else:
                     send(src, owned.at[y], fs.at[dy * NC + dc], fr, at(z, to, core))
 
-    for dy in range(1, NY):
-        wait(shares.at[0], p1s.at[dy])
-    for i, (src, dst) in enumerate(weights):
-        wait(src.at[0], ws.at[i])
-    for j in range(BLOCKS):
-        for way in range(2):
-            for h in range(len(ag[j][way])):
-                wait(rows.at[j, 0], ags.at[j, way, h])
-            for h in range(len(rs[j][way])):
-                wait(leaving.at[j, way, h], rss.at[j, way, h])
-        for i, way in enumerate((None, 1 - HEAVY[j], HEAVY[j])):
-            if way is None or short(ag, j, way):
-                wait(rows.at[j, 0], zcs.at[j, i])
-        for i, way in enumerate((1 - HEAVY[j], None, HEAVY[j])):
-            if way is None or short(rs, j, way):
-                wait(leaving_z.at[j, i], zss.at[j, i])
-        if j > 0:
-            wait(summed.at[j], rts.at[j])
+    wait(summed.at[1], rts.at[1])
+    wait(summed.at[2], rts.at[2])
+    wait(summed.at[3], rts.at[3])
 
     @pl.when(is_home)
     def _():
-        for i in range(1, 2 * BLOCKS):
-            wait(packed.at[0], p3s.at[i])
         for i in range(1, NY * NC):
             wait(mixed.at[0], fs.at[i])
 
     @pl.when(jnp.logical_not(is_home))
     def _():
-        wait(shares.at[0], p1s.at[0])
         wait(summed.at[0], rts.at[0])
 
     wait(owned, fr)
@@ -440,7 +445,7 @@
             pltpu.VMEM((EXPERTS, ROWS, ROWS), bf16),
             pltpu.VMEM((EXPERTS, ROWS, ROWS), bf16),
             pltpu.VMEM((EXPERTS, ROWS, 128), f32),
-            pltpu.VMEM((2 * BLOCKS, CAP, share), bf16),
+            pltpu.VMEM((2, EXPERTS, CAP, share), bf16),
             pltpu.VMEM((BLOCKS, NY, CAP, share), bf16),
             pltpu.VMEM((BLOCKS, CAP, NC * hid), bf16),
             pltpu.VMEM((BLOCKS, NY, CAP, share), f32),

time: 72.4 us -> 73.3 us (1.012)
  Pallas kernels: 70.8 us -> 71.7 us
    pallas_call x1, Pallas kernels: 70.8 us -> 71.7 us  [local(): pl.pallas_call(kernel, out_shape=jax.ShapeDtypeStruct((tok_dev, width), b...]
where the time goes in v5:
time: 73.3 us; the launch traced here: 73.1 us
  Pallas kernels  71.7 us (98%)
  local copies, waits for them, and re-layouts  1.42 us (2%)
    pallas_call x1, Pallas kernels, local(): pl.pallas_call(kernel, out_shape=jax.ShapeDtypeStruct((tok_dev, width), b...  71.7 us

profile of v5, /device:TPU:1, one launch (start us, length us, event | category | flops | bytes accessed | tf_op | source)
XLA Modules:
  0.0 73.1 jit_solution(13100562671669633203)
XLA Ops:
  0.0 71.7 %moe.1 = bf16[8,3072]{1,0:T(8,128)(2,1)} custom-call(bf16[8,3072]{1,0:T(8,128)(2,1)} %tok_in.1, s32[2,128]{1,0:T(2,128)} %bitcast.2, f32[2,128]{1,0:T(2,128)} %bitcast.3, bf16[1,3072,256]{2,1,0:T(8,128)(2,1)} %wg.1, bf16[1,3072,256]{2,1,0:T(8,128)(2,1)} %wu.1, bf16[1,256,3072]{2,1,0:T(8,128)(2,1)} %wd.1), custom_call_target="tpu_custom_call" | custom-call | tf_op jit(solution)/shard_map/moe/pallas_call | solution.py:431
  71.7 1.4 %copy.8 = bf16[8,3072]{1,0:T(8,128)(2,1)} copy(bf16[8,3072]{1,0:T(8,128)(2,1)} %moe.1) | data formatting | bytes 98304

commit v6 on v5

--- a/solution.py
+++ b/solution.py
@@ -19,78 +19,78 @@
 HEAVY = (0, 1, 0, 1)
 
 
-GROUPS = ((0, 2), (1, 3))
+GROUPS = ((1, 3), (0, 2))
 GATHER = (((0, 1, 2), (0, 1)), ((0, 1), (0, 1, 2)), ((0, 1, 2), (0, 1)), ((0, 1), (0, 1, 2)))
-SCATTER = (((0, 1, 2), (0, 1)), ((0, 1), (0, 1)), ((0, 1, 2), (0, 1)), ((0, 1), (0, 1)))
+SCATTER = (((0, 1, 2), (0, 1)), ((0, 1), (0, 1, 2)), ((0, 1, 2), (0, 1)), ((0, 1), (0, 1, 2)))
 ORDER = (
+    ("ag", 3, 0, 1),
+    ("zc", 3),
+    ("ag", 3, 1, 1),
     ("ag", 0, 0, 1),
+    ("zc", 0),
     ("ag", 0, 1, 1),
-    ("prep",),
-    ("zc", 0),
-    ("ag", 2, 0, 1),
-    ("ag", 2, 1, 1),
-    ("zc", 2),
-    ("ag", 0, 0, 2),
     ("ag", 1, 1, 1),
     ("ag", 1, 0, 1),
-    ("ag", 3, 1, 1),
-    ("ag", 2, 0, 2),
-    ("ag", 0, 1, 2),
-    ("ag", 0, 0, 3),
-    ("zf", 2),
+    ("ag", 2, 0, 1),
+    ("zc", 1),
+    ("zf", 3),
+    ("ag", 3, 0, 2),
+    ("ag", 3, 1, 2),
+    ("ag", 2, 1, 1),
     ("zf", 0),
     ("ag", 1, 1, 2),
-    ("ag", 3, 0, 1),
-    ("zc", 1),
+    ("prep",),
+    ("ag", 0, 0, 2),
+    ("zf", 1),
+    ("ag", 3, 1, 3),
+    ("ag", 2, 0, 2),
+    ("ag", 1, 0, 2),
+    ("zf", 2),
+    ("ag", 1, 1, 3),
+    ("ag", 0, 0, 3),
+    ("ag", 0, 1, 2),
+    ("zc", 2),
+    ("ag", 2, 0, 3),
     ("ag", 2, 1, 2),
-    ("ag", 2, 0, 3),
-    ("zc", 3),
-    ("ag", 1, 0, 2),
-    ("zf", 1),
-    ("ag", 3, 1, 2),
-    ("ag", 1, 1, 3),
-    ("zf", 3),
     ("up", 0, 0),
-    ("ag", 3, 0, 2),
-    ("ag", 3, 1, 3),
     ("up", 0, 1),
     ("down", 0, 0),
     ("down", 0, 1),
-    ("zt", 0),
-    ("rs", 0, 1, 2),
-    ("rs", 2, 1, 2),
-    ("rs", 2, 0, 3),
-    ("zs", 2),
-    ("zs", 0),
-    ("rs", 0, 0, 3),
+    ("rs", 3, 1, 3),
+    ("rs", 1, 0, 2),
+    ("zs", 3),
+    ("rs", 3, 0, 2),
+    ("rs", 1, 1, 3),
+    ("zt", 1),
+    ("zs", 1),
     ("up", 1, 0),
     ("up", 1, 1),
     ("down", 1, 0),
+    ("rs", 3, 1, 2),
     ("down", 1, 1),
-    ("rs", 1, 0, 2),
-    ("zu", 3),
+    ("rs", 0, 0, 3),
+    ("rs", 2, 0, 3),
+    ("rs", 2, 1, 2),
+    ("rs", 1, 0, 1),
+    ("rs", 1, 1, 2),
+    ("zt", 3),
+    ("zs", 2),
+    ("rs", 3, 0, 1),
+    ("rs", 0, 1, 2),
+    ("rs", 3, 1, 1),
+    ("zs", 0),
+    ("zt", 2),
     ("rs", 2, 0, 2),
-    ("zs", 1),
-    ("rs", 3, 0, 2),
-    ("rs", 3, 1, 2),
-    ("zu", 1),
+    ("rs", 0, 0, 2),
+    ("rs", 1, 1, 1),
+    ("zt", 0),
+    ("rs", 2, 1, 1),
     ("rs", 0, 1, 1),
-    ("zs", 3),
-    ("rs", 0, 0, 2),
-    ("rs", 1, 1, 2),
-    ("rs", 2, 1, 1),
-    ("zt", 1),
     ("rs", 2, 0, 1),
-    ("rs", 3, 1, 1),
-    ("rs", 3, 0, 1),
-    ("zt", 3),
-    ("rs", 1, 0, 1),
-    ("rs", 1, 1, 1),
+    ("fin", 3),
     ("rs", 0, 0, 1),
-    ("zt", 2),
+    ("fin", 1),
     ("fin", 2),
-    ("fin", 3),
-    ("fin", 1),
     ("fin", 0),
 )
 
@@ -194,7 +194,7 @@
             packed[i] = jnp.dot(
                 every, block[:, i * share:(i + 1) * share], preferred_element_type=jnp.float32
             ).reshape(EXPERTS, CAP, share).astype(jnp.bfloat16)
-        for j, k in ((0, 0), (0, 1), (2, 1), (3, 0), (3, 1), (2, 0), (1, 1), (1, 0)):
+        for j, k in ((0, 0), (3, 0), (3, 1), (1, 1), (1, 0), (2, 0), (0, 1), (2, 1)):
             to = ring(z - turn * OFFSETS[0][j], NZ) if k == 0 else ring(z + turn * OFFSETS[1][j], NZ)
             src = packed.at[j // 2, to // (NZ // EXPERTS)]
             slot = k * BLOCKS + j

time: 73.3 us -> 73.5 us (level)
  no operation moved by 1% of the time
where the time goes in v6:
time: 73.5 us; the launch traced here: 73.3 us
  Pallas kernels  71.9 us (98%)
  local copies, waits for them, and re-layouts  1.42 us (2%)
    pallas_call x1, Pallas kernels, local(): pl.pallas_call(kernel, out_shape=jax.ShapeDtypeStruct((tok_dev, width), b...  71.9 us

profile of v6, /device:TPU:1, one launch (start us, length us, event | category | flops | bytes accessed | tf_op | source)
XLA Modules:
  0.0 73.3 jit_solution(17066963520347492241)
XLA Ops:
  0.0 71.9 %moe.1 = bf16[8,3072]{1,0:T(8,128)(2,1)} custom-call(bf16[8,3072]{1,0:T(8,128)(2,1)} %tok_in.1, s32[2,128]{1,0:T(2,128)} %bitcast.2, f32[2,128]{1,0:T(2,128)} %bitcast.3, bf16[1,3072,256]{2,1,0:T(8,128)(2,1)} %wg.1, bf16[1,3072,256]{2,1,0:T(8,128)(2,1)} %wu.1, bf16[1,256,3072]{2,1,0:T(8,128)(2,1)} %wd.1), custom_call_target="tpu_custom_call" | custom-call | tf_op jit(solution)/shard_map/moe/pallas_call | solution.py:431
  71.9 1.4 %copy.8 = bf16[8,3072]{1,0:T(8,128)(2,1)} copy(bf16[8,3072]{1,0:T(8,128)(2,1)} %moe.1) | data formatting | bytes 98304
